TPU v7x, 32 devices: a whole 2x2x4 slice. The times are simulated.
32 devices in a mesh: nodes: 16 (over z, y, core), feat: 2 (over x).
Axes of the slice: x: 2, y: 2, z: 4, core: 2. Of those that a mesh axis runs over, the one named last changes fastest.
Arguments:
- node_feats: float32 [4096, 768], P(('nodes', 'feat')), may hold values from -6 to 6
- rel_weights: float32 [5, 512, 768], P(None, 'feat'), may hold values from -0.21875 to 0.21875
- self_weight: float32 [512, 768], P('feat'), may hold values from -0.21875 to 0.21875
- cotangent: float32 [512, 4096], P('feat', 'nodes'), may hold values from -6 to 6
- tile_values: bfloat16 [16, 5, 6, 128, 128], P('nodes'), may hold values from 0 to 0.049804688
- tile_peer: int32 [16, 5, 6], P('nodes'), may hold values from 0 to 15, as said below
- tile_slot: int32 [16, 5, 6], P('nodes'), may hold values from 0 to 1, as said below
- tile_target: int32 [16, 5, 6], P('nodes'), may hold values from 0 to 1
- tile_count: int32 [16, 5], P('nodes'), may hold values from 3 to 6, as said below
- send_mask: int32 [16, 16, 10], P('nodes'), may hold values from 0 to 1, as said below
Outputs:
- layer_out: float32 [512, 4096], P('feat', 'nodes')
- feat_grad: float32 [4096, 768], P(('nodes', 'feat'))
- rel_grad: float32 [5, 512, 768], P(None, 'feat')
- self_grad: float32 [512, 768], P('feat')
Inputs may be any that keep to these rules, and one draw needn't show every extreme that they name: `tile_count`: every draw has some partition and relation with 6 live tiles. For a live tile (p, r, t), send_mask[tile_peer[p, r, t], p] holds more than tile_slot[p, r, t] ones, and the named slot's column lies in relation r's columns r * 2 to r * 2 + 1; the live tiles of a partition name distinct slots. Entries of tiles that are not live are arbitrary within the range. `tile_peer`: entries of tiles that are not live are arbitrary within the range. `send_mask`: each sending and receiving pair of partitions has at most 2 ones, and 2 are reached in every draw; every one is named by exactly one live tile.
All inputs are finite; a program needn't handle non-finite values.
Results may differ from a plain program's by a relative error of at most 0.0003.
Values sent between devices are 32-bit elements; how exact they have to be, the bound alone decides.
A program may use at most 128 MiB of HBM per device.

v0:
```python
import functools

import jax
import jax.numpy as jnp
from jax import lax
from jax.experimental import pallas as pl
from jax.experimental.pallas import tpu as pltpu
from jax.sharding import PartitionSpec as P

TILE = 128
CAP = 2


def slot_exchange(
    node_feats,
    rel_weights,
    self_weight,
    cotangent,
    tile_values,
    tile_peer,
    tile_slot,
    tile_target,
    tile_count,
    send_mask,
):
    highest = lax.Precision.HIGHEST
    relations = rel_weights.shape[0]
    out_share = rel_weights.shape[1]
    part_rows = cotangent.shape[1]
    blocks = part_rows // TILE
    parts = lax.axis_size("nodes")
    slot_steps = tile_values.shape[2]
    combined = relations * blocks
    gathered = lax.all_gather(node_feats, "feat", axis=0, tiled=True)
    hidden = jnp.einsum("rfi,ni->rfn", rel_weights, gathered, precision=highest)
    self_part = jnp.einsum("fi,ni->fn", self_weight, gathered, precision=highest)
    hidden_blocks = (
        hidden.reshape(relations, out_share, blocks, TILE)
        .transpose(0, 2, 1, 3)
        .reshape(combined, out_share, TILE)
    )
    mask_rows = send_mask[0]
    slot_rank = jnp.cumsum(mask_rows, axis=1) - 1
    slot_ids = jnp.arange(CAP, dtype=jnp.int32)
    chooser = (
        (mask_rows[:, :, None] == 1) & (slot_rank[:, :, None] == slot_ids[None, None, :])
    ).astype(jnp.float32)
    outgoing = jnp.einsum("pcs,cfk->psfk", chooser, hidden_blocks, precision=highest)
    arrived = lax.all_to_all(outgoing, "nodes", split_axis=0, concat_axis=0, tiled=True)
    position = (tile_peer[0] * CAP + tile_slot[0]).reshape(-1)
    alive = (
        (jnp.arange(slot_steps, dtype=jnp.int32)[None, :] < tile_count[0][:, None])
        .reshape(-1)
        .astype(jnp.float32)
    )
    pieces = arrived.reshape(parts * CAP, out_share, TILE)[position] * alive[:, None, None]
    weights = tile_values[0].reshape(relations * slot_steps, TILE, TILE)
    contrib = jnp.einsum(
        "tfu,tvu->tfv", pieces, weights, precision=highest, preferred_element_type=jnp.float32
    )
    targets = (
        tile_target[0].reshape(-1)[:, None] == jnp.arange(blocks, dtype=jnp.int32)[None, :]
    ).astype(jnp.float32)
    summed = jnp.einsum("tb,tfv->fbv", targets, contrib, precision=highest).reshape(
        out_share, part_rows
    )
    layer_out = summed + self_part
    grad_blocks = cotangent.reshape(out_share, blocks, TILE)
    picked = jnp.einsum("tb,fbv->tfv", targets, grad_blocks, precision=highest)
    returned = jnp.einsum(
        "tfv,tvu->tfu", picked, weights, precision=highest, preferred_element_type=jnp.float32
    )
    placing = (position[:, None] == jnp.arange(parts * CAP, dtype=jnp.int32)[None, :]).astype(
        jnp.float32
    ) * alive[:, None]
    going_back = jnp.einsum("tq,tfu->qfu", placing, returned, precision=highest).reshape(
        parts, CAP, out_share, TILE
    )
    came_back = lax.all_to_all(going_back, "nodes", split_axis=0, concat_axis=0, tiled=True)
    source_grads = jnp.einsum("pcs,psfk->cfk", chooser, came_back, precision=highest)
    grad_hidden = (
        source_grads.reshape(relations, blocks, out_share, TILE)
        .transpose(0, 2, 1, 3)
        .reshape(relations, out_share, part_rows)
    )
    rel_local = jnp.einsum("rfn,ni->rfi", grad_hidden, gathered, precision=highest)
    self_local = jnp.dot(cotangent, gathered, precision=highest)
    rel_total, self_total = lax.psum((rel_local, self_local), "nodes")
    factor = float(part_rows * parts) ** (-0.5)
    term = jnp.einsum("rfn,rfi->ni", grad_hidden, rel_weights, precision=highest)
    feat_grad = lax.psum_scatter(
        term + jnp.einsum("fn,fi->ni", cotangent, self_weight, precision=highest),
        "feat",
        scatter_dimension=0,
        tiled=True,
    )
    return (layer_out, feat_grad, rel_total * factor, self_total * factor)


LANES = 128
MASK_ROWS = 8
VMEM_LIMIT = 60 * 1024 * 1024
MESH = pl.DeviceIdType.MESH
STEPS = 4


def bit_of(value, weight):
    return lax.rem(lax.div(value, jnp.int32(weight)), jnp.int32(2))


def place():
    node = lax.axis_index("nodes")
    share = lax.axis_index("feat")
    bits = [bit_of(node, 8), bit_of(node, 4), bit_of(node, 2), bit_of(node, 1)]
    rank = bits[0] + 2 * bits[1] + 4 * bits[2] + 8 * bits[3]
    partners = [
        (node + weight * (1 - 2 * bit), share) for weight, bit in zip((8, 4, 2, 1), bits)
    ]
    across = (node, 1 - share)
    return rank, bits, share, partners, across


def rank_of(node):
    return node // 8 % 2 + 2 * (node // 4 % 2) + 4 * (node // 2 % 2) + 8 * (node % 2)


def greet(devices):
    barrier = pltpu.get_barrier_semaphore()
    for device in devices:
        pl.semaphore_signal(barrier, inc=1, device_id=device, device_id_type=MESH)
    pl.semaphore_wait(barrier, len(devices))


class Sender:
    def __init__(self, send_sems, recv_sems):
        self.send_sems, self.recv_sems, self.used, self.copies = send_sems, recv_sems, 0, []

    def start(self, source, target, device):
        copy = pltpu.make_async_remote_copy(
            src_ref=source,
            dst_ref=target,
            send_sem=self.send_sems.at[self.used],
            recv_sem=self.recv_sems.at[self.used],
            device_id=device,
            device_id_type=MESH,
        )
        self.used += 1
        self.copies.append(copy)
        copy.start()
        return copy

    def finish(self):
        for copy in self.copies:
            copy.wait_send()


def rows(start, count):
    return pl.ds(pl.multiple_of(start, 8), count)


def columns(start, count):
    return pl.ds(pl.multiple_of(start, LANES), count)


def gather_kernel(
    feats, rel_weights, self_weight, cotangent, mask, gathered, got_weights, got_cotangent,
    send_sems, recv_sems, own_sems,
):
    rank, bits, share, partners, across = place()
    core = bits[3]
    sibling = partners[3]
    chunks = gathered.shape[0]
    half = chunks * LANES
    seg = gathered.shape[1] // 16
    relations = rel_weights.shape[0]
    own_rows = feats.shape[0]
    base = rank * seg
    own = []
    for k in range(chunks):
        for count, (source, target) in enumerate(
            (
                (
                    feats.at[:, columns(share * half + k * LANES, LANES)],
                    gathered.at[k, rows(base + share * own_rows, own_rows)],
                ),
                (mask, gathered.at[k, rows(base + 2 * own_rows, MASK_ROWS)]),
            )
        ):
            copy = pltpu.make_async_copy(source, target, own_sems.at[2 * k + count])
            copy.start()
            own.append(copy)
    greet(partners + [across])
    sender = Sender(send_sems, recv_sems)
    far = (1 - share) * half
    crossing = [
        sender.start(
            feats.at[:, columns(far + k * LANES, LANES)],
            gathered.at[k, rows(base + share * own_rows, own_rows)],
            across,
        )
        for k in range(chunks)
    ]
    cotangent_copy = sender.start(cotangent, got_cotangent, across)
    pairs = (relations + 1) // 2
    lower = [
        sender.start(
            rel_weights.at[core * (pairs - 1) + j, :, columns(far, half)],
            got_weights.at[core * (pairs - 1) + j],
            across,
        )
        for j in range(pairs - 1)
    ]
    weight_rows = rel_weights.shape[1] // 2
    lower.append(
        sender.start(
            rel_weights.at[relations - 1, rows(core * weight_rows, weight_rows), columns(far, half)],
            got_weights.at[relations - 1, rows(core * weight_rows, weight_rows)],
            across,
        )
    )
    lower.append(
        sender.start(
            self_weight.at[rows(core * weight_rows, weight_rows), columns(far, half)],
            got_weights.at[relations, rows(core * weight_rows, weight_rows)],
            across,
        )
    )
    for copy in own:
        copy.wait()
    last = list(crossing)
    for wave in range(chunks + STEPS):
        for k in range(chunks):
            step = wave - k
            if step < 0 or step > STEPS:
                continue
            last[k].wait_recv()
            if step == STEPS:
                continue
            size = 1 << step
            held = gathered.at[k, rows(lax.div(rank, jnp.int32(size)) * (size * seg), size * seg)]
            last[k] = sender.start(held, held, partners[step])
    forwarded = []
    for j, copy in enumerate(lower):
        copy.wait_recv()
        if j < pairs - 1:
            block = got_weights.at[core * (pairs - 1) + j]
        else:
            block = got_weights.at[j + pairs - 1, rows(core * weight_rows, weight_rows)]
        forwarded.append(sender.start(block, block, sibling))
    cotangent_copy.wait_recv()
    for copy in forwarded:
        copy.wait_recv()
    sender.finish()


def parts_of(value):
    high = value.astype(jnp.bfloat16)
    return high, (value - high.astype(jnp.float32)).astype(jnp.bfloat16)


def product(left, right, dims):
    def one(a, b):
        return lax.dot_general(a, b, (dims, ((), ())), preferred_element_type=jnp.float32)

    return one(left[0], right[0]) + (one(left[0], right[1]) + one(left[1], right[0]))


def exact_product(left, right, dims):
    high, low = parts_of(right)

    def one(b):
        return lax.dot_general(left, b, (dims, ((), ())), preferred_element_type=jnp.float32)

    return one(high) + one(low)


def compute_kernel(
    counts, ranks, blocks, targets, own_rank, tiles, gathered, near_weights, far_weights,
    near_cotangent, far_cotangent, near_out, far_out, feat_parts, rel_parts, mixed, mixed_grad,
):
    relations, slots = ranks.shape
    chunks = gathered.shape[0]
    part_rows = near_cotangent.shape[1]
    seg = gathered.shape[1] // 16
    near = parts_of(near_cotangent[...])
    far = parts_of(far_cotangent[...])
    near_t = parts_of(near_cotangent[...].T)
    far_t = parts_of(far_cotangent[...].T)
    feat_parts[...] = jnp.zeros_like(feat_parts)
    share_rows = near_cotangent.shape[0] // 16
    near_out[...] = jnp.zeros_like(near_out)
    far_out[...] = jnp.zeros_like(far_out)

    def weight_parts(r):
        return parts_of(near_weights[r]), parts_of(far_weights[r])

    @pl.loop(0, relations + 1)
    def _(r):
        @pl.when(r < relations)
        def _():
            mixed[...] = jnp.zeros_like(mixed)

            @pl.loop(0, counts[lax.min(r, relations - 1)])
            def _(t):
                start = ranks[r, t] * seg + blocks[r, t] * TILE
                piece = jnp.concatenate(
                    [gathered[k, rows(start, TILE), :] for k in range(chunks)], axis=1
                )
                there = rows(targets[r, t] * TILE, TILE)
                mixed[there, :] += exact_product(tiles[r * slots + t], piece, ((1,), (0,)))

        own_start = own_rank[0] * seg

        @pl.when(r == relations)
        def _():
            for k in range(chunks):
                mixed[:, k * LANES : (k + 1) * LANES] = gathered[k, rows(own_start, part_rows), :]

        near_w, far_w = weight_parts(r)
        z = parts_of(mixed[...])
        near_out[...] += product(near_w, z, ((1,), (1,)))
        far_out[...] += product(far_w, z, ((1,), (1,)))
        for which, grad in enumerate((near, far)):
            result = product(grad, z, ((1,), (0,)))
            for q in range(16):
                for k in range(chunks):
                    rel_parts[
                        k, rows(q * 2 * 6 * share_rows + which * 6 * share_rows + r * share_rows, share_rows), :
                    ] = result[q * share_rows : (q + 1) * share_rows, k * LANES : (k + 1) * LANES]
        mixed_grad[...] = product(near_t, near_w, ((1,), (0,))) + product(
            far_t, far_w, ((1,), (0,))
        )

        @pl.when(r < relations)
        def _():
            @pl.loop(0, counts[lax.min(r, relations - 1)])
            def _(t):
                start = ranks[r, t] * part_rows + blocks[r, t] * TILE
                there = rows(targets[r, t] * TILE, TILE)
                back = exact_product(tiles[r * slots + t], mixed_grad[there, :], ((0,), (0,)))
                for k in range(chunks):
                    feat_parts[k, rows(start, TILE), :] += back[:, k * LANES : (k + 1) * LANES]

        @pl.when(r == relations)
        def _():
            for k in range(chunks):
                feat_parts[k, rows(own_rank[0] * part_rows, part_rows), :] += mixed_grad[
                    :, k * LANES : (k + 1) * LANES
                ]


def add_rows(target, target_start, source, source_start, count):
    block = 64

    def body(i, carry):
        there = rows(target_start + i * block, block)
        target[there, :] = target[there, :] + source[rows(source_start + i * block, block), :]
        return carry

    lax.fori_loop(0, count // block, body, 0)


def reduce_kernel(
    feat_parts, rel_parts, far_out, rel_total, feat_total, got_out,
    feat_sums, rel_sums, send_sems, recv_sems, own_sems,
):
    rank, bits, share, partners, across = place()
    chunks = feat_parts.shape[0]
    feat_seg = feat_parts.shape[1] // 16
    rel_seg = rel_parts.shape[1] // 16
    own_rows = feat_seg // 2
    part = rel_seg // 2
    greet(partners + [across])
    sender = Sender(send_sems, recv_sems)
    out_copy = sender.start(far_out, got_out, across)
    local_copies = []

    def chain(kind, k):
        inputs, sums, seg = (
            (rel_parts, rel_sums, rel_seg) if kind == "rel" else (feat_parts, feat_sums, feat_seg)
        )
        copy = None
        for step in (3, 2, 1, 0, -1):
            if copy is not None:
                copy.wait_recv()
                size = 1 << (step + 1)
                mine = size * seg * bit_of(rank, size)
                if step == 2:
                    add_rows(
                        sums.at[k], (size - 1) * seg, inputs.at[k],
                        lax.div(rank, jnp.int32(8)) * (8 * seg), size * seg,
                    )
                else:
                    add_rows(
                        sums.at[k], (size - 1) * seg, sums.at[k],
                        (2 * size - 1) * seg + mine, size * seg,
                    )
            if step < 0:
                break
            size = 1 << step
            other = 1 - bit_of(rank, size)
            if step == 3:
                source = inputs.at[k, rows(other * (8 * seg), 8 * seg)]
            else:
                source = sums.at[
                    k, rows((2 * size - 1) * seg + other * (size * seg), size * seg)
                ]
            copy = sender.start(
                source, sums.at[k, rows((size - 1) * seg, size * seg)], partners[step]
            )
            yield
        where = share * chunks + k
        if kind == "feat":
            cross = sender.start(
                sums.at[k, rows((1 - share) * own_rows, own_rows)], feat_total.at[where], across
            )
            local = pltpu.make_async_copy(
                sums.at[k, rows(share * own_rows, own_rows)],
                feat_total.at[where],
                own_sems.at[chunks + k],
            )
            local.start()
            local_copies.append(local)
            yield
            cross.wait_recv()
            return
        cross = sender.start(
            sums.at[k, pl.ds(part, part)], rel_total.at[where, rows(rank * part, part)], across
        )
        local = pltpu.make_async_copy(
            sums.at[k, pl.ds(0, part)],
            rel_total.at[where, rows(rank * part, part)],
            own_sems.at[k],
        )
        local.start()
        local.wait()
        waiting = [None, cross]
        for wave in range(STEPS + 2):
            for piece in range(2):
                step = wave - piece
                if step < 0 or step > STEPS:
                    continue
                if waiting[piece] is not None:
                    waiting[piece].wait_recv()
                if step == STEPS:
                    continue
                size = 1 << step
                index = (share if piece == 0 else 1 - share) * chunks + k
                held = rel_total.at[
                    index, rows(lax.div(rank, jnp.int32(size)) * (size * part), size * part)
                ]
                waiting[piece] = sender.start(held, held, partners[step])
            yield

    chains = [chain("rel", k) for k in range(chunks)] + [chain("feat", k) for k in range(chunks)]
    active = []
    while chains or active:
        if chains:
            active.append(chains.pop(0))
        for one in list(active):
            if next(one, "end") == "end":
                active.remove(one)
    out_copy.wait_recv()
    for local in local_copies:
        local.wait()
    sender.finish()


def vmem(count):
    return [pl.BlockSpec(memory_space=pltpu.VMEM)] * count


def plane_gather(
    node_feats, rel_weights, self_weight, cotangent, tile_values, tile_peer, tile_slot,
    tile_target, tile_count, send_mask,
):
    f32 = jnp.float32
    relations, out_share, features = rel_weights.shape
    part_rows = cotangent.shape[1]
    own_rows = node_feats.shape[0]
    blocks = part_rows // TILE
    parts = lax.axis_size("nodes")
    half = features // 2
    chunks = half // LANES
    slots = tile_values.shape[2]
    seg = part_rows + MASK_ROWS
    node = lax.axis_index("nodes")
    share = lax.axis_index("feat")
    mask = send_mask[0].astype(f32).reshape(-1)
    mask = jnp.pad(mask, (0, MASK_ROWS * LANES - mask.shape[0])).reshape(MASK_ROWS, LANES)
    shape = jax.ShapeDtypeStruct
    gathered, far_weights, far_cotangent = pl.pallas_call(
        gather_kernel,
        out_shape=(
            shape((chunks, parts * seg, LANES), f32),
            shape((relations + 1, out_share, half), f32),
            shape((out_share, part_rows), f32),
        ),
        in_specs=vmem(5),
        out_specs=tuple(vmem(3)),
        scratch_shapes=[
            pltpu.SemaphoreType.DMA((32,)),
            pltpu.SemaphoreType.DMA((32,)),
            pltpu.SemaphoreType.DMA((2 * chunks,)),
        ],
        compiler_params=pltpu.CompilerParams(
            collective_id=0, has_side_effects=True, vmem_limit_bytes=VMEM_LIMIT
        ),
        name="gather_nodes",
    )(node_feats, rel_weights, self_weight, cotangent, mask)
    masks = gathered[0].reshape(parts, seg, LANES)[:, part_rows:].reshape(parts, -1)
    columns_all = relations * blocks
    masks = masks[:, : parts * columns_all].reshape(parts, parts, columns_all)
    to_me = jnp.sum(
        masks * (jnp.arange(parts) == node).astype(f32)[None, :, None], axis=1
    ).astype(jnp.int32)
    peer = tile_peer[0]
    peer_rank = rank_of(peer)
    picked = jnp.sum(
        jnp.where(peer_rank[:, :, None, None] == jnp.arange(parts)[None, None, :, None], to_me, 0),
        axis=2,
    )
    order = jnp.cumsum(picked, axis=2) - 1
    found = (picked == 1) & (order == tile_slot[0][:, :, None])
    column = jnp.sum(jnp.where(found, jnp.arange(columns_all)[None, None, :], 0), axis=2)
    block = (column % blocks).astype(jnp.int32)
    near_weights = lax.dynamic_slice_in_dim(
        jnp.concatenate([rel_weights, self_weight[None]]), share * half, half, 2
    )
    own_rank = rank_of(node).astype(jnp.int32).reshape(1)
    rel_rows = (relations + 1) * out_share // parts
    smem = [pl.BlockSpec(memory_space=pltpu.SMEM)] * 5
    near_out, far_out, feat_parts, rel_parts = pl.pallas_call(
        compute_kernel,
        out_shape=(
            shape((out_share, part_rows), f32),
            shape((out_share, part_rows), f32),
            shape((chunks, parts * part_rows, LANES), f32),
            shape((chunks, parts * 2 * rel_rows, LANES), f32),
        ),
        in_specs=smem + vmem(6),
        out_specs=tuple(vmem(4)),
        scratch_shapes=[pltpu.VMEM((part_rows, half), f32), pltpu.VMEM((part_rows, half), f32)],
        compiler_params=pltpu.CompilerParams(vmem_limit_bytes=VMEM_LIMIT),
        name="local_products",
    )(
        tile_count[0], peer_rank, block, tile_target[0], own_rank,
        tile_values[0].reshape(relations * slots, TILE, TILE),
        gathered, near_weights, far_weights, cotangent, far_cotangent,
    )
    rel_total, feat_total, got_out = pl.pallas_call(
        reduce_kernel,
        out_shape=(
            shape((2 * chunks, parts * rel_rows, LANES), f32),
            shape((2 * chunks, own_rows, LANES), f32),
            shape((out_share, part_rows), f32),
        ),
        in_specs=vmem(3),
        out_specs=tuple(vmem(3)),
        scratch_shapes=[
            pltpu.VMEM((chunks, 15 * part_rows, LANES), f32),
            pltpu.VMEM((chunks, 15 * 2 * rel_rows, LANES), f32),
            pltpu.SemaphoreType.DMA((72,)),
            pltpu.SemaphoreType.DMA((72,)),
            pltpu.SemaphoreType.DMA((2 * chunks,)),
        ],
        compiler_params=pltpu.CompilerParams(
            collective_id=1, has_side_effects=True, vmem_limit_bytes=VMEM_LIMIT
        ),
        name="reduce_grads",
    )(feat_parts, rel_parts, far_out)
    layer_out = near_out + got_out
    feat_grad = feat_total.transpose(1, 0, 2).reshape(own_rows, features)
    factor = float(part_rows * parts) ** (-0.5)
    totals = rel_total.reshape(2 * chunks, parts, relations + 1, out_share // parts, LANES)
    totals = totals.transpose(2, 1, 3, 0, 4).reshape(relations + 1, out_share, features) * factor
    return (layer_out, feat_grad, totals[:relations], totals[relations])


def local(node_feats, rel_weights, self_weight, cotangent, *tiles):
    relations, out_share, features = rel_weights.shape
    parts, shares = lax.axis_size("nodes"), lax.axis_size("feat")
    fits = (
        parts == 16
        and shares == 2
        and relations == 5
        and out_share == 256
        and cotangent.shape[1] == 2 * TILE
        and features == 6 * LANES
    )
    plan = plane_gather if fits else slot_exchange
    return plan(node_feats, rel_weights, self_weight, cotangent, *tiles)


def solution(mesh):
    return jax.shard_map(
        local,
        mesh=mesh,
        in_specs=(
            P(("nodes", "feat"), None),
            P(None, "feat", None),
            P("feat", None),
            P("feat", "nodes"),
            P("nodes", None, None, None, None),
            P("nodes", None, None),
            P("nodes", None, None),
            P("nodes", None, None),
            P("nodes", None),
            P("nodes", None, None),
        ),
        out_specs=(
            P("feat", "nodes"),
            P(("nodes", "feat"), None),
            P(None, "feat", None),
            P("feat", None),
        ),
        check_vma=False,
    )
```

profile of v0, /device:TPU:1, one launch (start us, length us, event | category | flops | bytes accessed | tf_op | source)
XLA Modules:
  0.0 236.5 jit_solution(6053702479624962390)
XLA Ops:
  0.7 0.7 fusion.6.ranks
  1.4 0.0 copy-start.1
  1.4 0.7 copy.83
  2.1 1.3 copy.82
  3.4 0.1 iota_compare_fusion
  3.5 0.7 convert_element_type.19
  4.2 0.1 copy.25
  4.3 0.1 convert_element_type.20
  4.4 0.6 pad_bitcast_fusion.mask
  5.0 3.1 %fusion.near_weights = f32[6,256,384]{2,1,0:T(8,128)} fusion(s32[]{:T(128)S(6)} %select_n.118, f32[5,256,768]{2,1,0:T(8,128)} %rel_weights.1, f32[1,256,768]{2,1,0:T(8,128)} %bitcast.70), kind=kLoop, calls=%fused_computation.3 | loop fusion | flops 589824 | bytes 7077892 | tf_op jit(solution)/shard_map/concatenate | solution.py:528
  8.1 69.9 %gather_nodes.1 = (f32[3,4224,128]{2,1,0:T(8,128)}, f32[6,256,384]{2,1,0:T(8,128)}, f32[256,256]{1,0:T(8,128)}) custom-call(f32[128,768]{1,0:T(8,128)} %feats.1, f32[5,256,768]{2,1,0:T(8,128)} %rel_weights.1, f32[256,768]{1,0:T(8,128)} %self_weight.1, f32[256,256]{1,0:T(8,128)} %near_cotangent.1, f32[8,128]{1,0:T(8,128)} %pad_bitcast_fusion.mask), custom_call_target="tpu_custom_call" | custom-call | tf_op jit(solution)/shard_map/gather_nodes/pallas_call | solution.py:492
  78.0 0.0 copy-done.1
  78.0 1.8 slice.19
  79.8 0.1 reshape.157
  79.9 0.1 multiply_reduce_fusion
  80.0 0.1 copy.26
  80.1 0.9 select_reduce_fusion
  81.1 0.6 add_select_fusion.blocks
  81.7 29.8 %local_products.1 = (f32[256,256]{1,0:T(8,128)}, f32[256,256]{1,0:T(8,128)}, f32[3,4096,128]{2,1,0:T(8,128)}, f32[3,3072,128]{2,1,0:T(8,128)}) custom-call(s32[5]{0:T(128)} %bitcast.80, s32[5,6]{1,0:T(8,128)} %copy-done.1, s32[5,6]{1,0:T(8,128)} %add_select_fusion.blocks, s32[5,6]{1,0:T(8,128)} %bitcast.78, s32[1]{0:T(128)} %bitcast.3.own_rank, ...), custom_call_target="tpu_custom_call" | custom-call | tf_op jit(solution)/shard_map/local_products/pallas_call | solution.py:533
  111.5 0.0 copy-start
  111.5 105.9 %reduce_grads.1 = (f32[6,1536,128]{2,1,0:T(8,128)}, f32[6,128,128]{2,1,0:T(8,128)}, f32[256,256]{1,0:T(8,128)}) custom-call(f32[3,4096,128]{2,1,0:T(8,128)} %get-tuple-element.18.feat_parts, f32[3,3072,128]{2,1,0:T(8,128)} %get-tuple-element.19.rel_parts, f32[256,256]{1,0:T(8,128)} %get-tuple-element.20.far_out), custom_call_target="tpu_custom_call" | custom-call | tf_op jit(solution)/shard_map/reduce_grads/pallas_call | solution.py:551
  217.3 0.0 copy-done
  217.3 1.7 add.120
  219.0 1.2 copy.28
  220.2 0.9 copy.30
  221.1 2.6 %broadcast_multiply_fusion = f32[6,1536,128]{2,1,0:T(8,128)S(1)} fusion(f32[6,1536,128]{2,1,0:T(8,128)} %get-tuple-element.23), kind=kLoop, calls=%fused_computation.4 | loop fusion | flops 1179648 | bytes 9437184 | tf_op jit(solution)/shard_map/mul | solution.py:576
  223.8 2.8 %copy.79 = f32[6,16,6,16,128]{4,0,3,1,2:T(8,128)S(1)} copy(f32[6,16,6,16,128]{4,3,2,1,0:T(8,128)S(1)} %bitcast.68) | data formatting | bytes 9437184 | tf_op jit(solution)/shard_map/mul | solution.py:576
  226.6 0.1 slice.28
  226.7 2.9 %slice.27 = f32[5,16,16,6,128]{4,3,2,1,0:T(8,128)} slice(f32[6,16,16,6,128]{4,3,2,1,0:T(8,128)S(1)} %bitcast.67), slice={[0:5], [0:16], [0:16], [0:6], [0:128]} | slice | bytes 7864320 | tf_op jit(solution)/shard_map/slice | solution.py:577
  229.6 5.8 %slice.23 = f32[5,256,768]{2,1,0:T(8,128)} reshape(f32[5,16,16,6,128]{4,3,2,1,0:T(8,128)} %slice.27) | data formatting | bytes 7864320 | tf_op jit(solution)/shard_map/slice | solution.py:577
  235.4 1.0 copy.80
  (7 shorter events, 0.1 us)
Async XLA Ops:
  1.4 76.6 %copy-start.1 = (s32[5,6]{1,0:T(8,128)}, s32[5,6]{1,0:T(8,128)S(1)}, u32[]{:S(2)}) copy-start(s32[5,6]{1,0:T(8,128)S(1)} %fusion.6.ranks) | copy-start | bytes 364
  111.5 105.9 %copy-start = (f32[256,256]{1,0:T(8,128)S(1)}, f32[256,256]{1,0:T(8,128)}, u32[]{:S(2)}) copy-start(f32[256,256]{1,0:T(8,128)} %get-tuple-element.17) | copy-start | bytes 786436
where the time goes:
time: 237 us; the launch traced here: 236 us
  Pallas kernels  206 us (87%)
  local copies, waits for them, and re-layouts  19.5 us (8%)
  other arithmetic  10.6 us (4%)
    pallas_call x1, Pallas kernels, plane_gather(): pl.pallas_call(reduce_kernel, out_shape=(shape((2 * chunks, parts * rel_r...  106 us
    pallas_call x1, Pallas kernels, plane_gather(): pl.pallas_call(gather_kernel, out_shape=(shape((chunks, parts * seg, LANE...  69.9 us
    pallas_call x1, Pallas kernels, plane_gather(): pl.pallas_call(compute_kernel, out_shape=(shape((out_share, part_rows), f...  29.8 us
    slice x3, local copies, waits for them, and re-layouts, plane_gather(): return (layer_out, feat_grad, totals[:relations], totals[relations])  8.83 us

commit v1 on v0

--- a/solution.py
+++ b/solution.py
@@ -121,7 +121,13 @@
 
 
 def rank_of(node):
-    return node // 8 % 2 + 2 * (node // 4 % 2) + 4 * (node // 2 % 2) + 8 * (node % 2)
+    z1, z0, y, core = (bit_of(node, weight) for weight in (8, 4, 2, 1))
+    return z1 + 2 * z0 + 4 * y + 8 * core
+
+
+def other_rank_of(node):
+    z1, z0, y, core = (bit_of(node, weight) for weight in (8, 4, 2, 1))
+    return z1 + 2 * y + 4 * z0 + 8 * core
 
 
 def greet(devices):
@@ -227,28 +233,50 @@
     )
     for copy in own:
         copy.wait()
-    last = list(crossing)
-    for wave in range(chunks + STEPS):
-        for k in range(chunks):
-            step = wave - k
-            if step < 0 or step > STEPS:
-                continue
-            last[k].wait_recv()
-            if step == STEPS:
-                continue
-            size = 1 << step
-            held = gathered.at[k, rows(lax.div(rank, jnp.int32(size)) * (size * seg), size * seg)]
-            last[k] = sender.start(held, held, partners[step])
-    forwarded = []
-    for j, copy in enumerate(lower):
-        copy.wait_recv()
+
+    def held(start, count):
+        return rows(start * seg, count * seg)
+
+    def send(k, start, count, step):
+        block = gathered.at[k, held(start, count)]
+        return sender.start(block, block, partners[step])
+
+    def forward(j):
+        lower[j].wait_recv()
         if j < pairs - 1:
             block = got_weights.at[core * (pairs - 1) + j]
         else:
             block = got_weights.at[j + pairs - 1, rows(core * weight_rows, weight_rows)]
         forwarded.append(sender.start(block, block, sibling))
+
+    forwarded = []
+    first, first_other = rank, rank + 1 - 2 * bits[0]
+    second = rank - bits[0]
+    second_other = second + 2 - 4 * bits[1]
+    third = second - 2 * bits[1]
+    third_other = third + 4 - 8 * bits[2]
+    by_z1, by_z0, by_y, by_core = [], [], [], []
+    for k in range(chunks):
+        crossing[k].wait_recv()
+        by_z1.append(send(k, first, 1, 0))
+        by_y.append([send(k, first, 1, 2)])
+    for k in range(chunks):
+        by_z1[k].wait_recv()
+        by_z0.append(send(k, second, 2, 1))
+        by_y[k].append(send(k, first_other, 1, 2))
+    for k in range(chunks):
+        by_z0[k].wait_recv()
+        by_y[k].append(send(k, second_other, 2, 2))
+        by_core.append(send(k, third, 4, 3))
+    for k in range(chunks):
+        for copy in by_y[k]:
+            copy.wait_recv()
+        by_core.append(send(k, third_other, 4, 3))
+        forward(k)
+    for j in range(chunks, len(lower)):
+        forward(j)
     cotangent_copy.wait_recv()
-    for copy in forwarded:
+    for copy in by_core + forwarded:
         copy.wait_recv()
     sender.finish()
 
@@ -275,77 +303,107 @@
 
 
 def compute_kernel(
-    counts, ranks, blocks, targets, own_rank, tiles, gathered, near_weights, far_weights,
-    near_cotangent, far_cotangent, near_out, far_out, feat_parts, rel_parts, mixed, mixed_grad,
+    counts, peers, slot_ids, targets, me, tiles, gathered, rel_weights, self_weight, far_weights,
+    near_cotangent, far_cotangent, near_out, far_out, feat_parts, rel_parts, masks, mask_sems,
 ):
-    relations, slots = ranks.shape
+    relations, slots = peers.shape
     chunks = gathered.shape[0]
-    part_rows = near_cotangent.shape[1]
+    half = chunks * LANES
+    out_share, part_rows = near_cotangent.shape
     seg = gathered.shape[1] // 16
+    blocks = 2
+    node, share = me[0], me[1]
+    copies = [
+        pltpu.make_async_copy(
+            gathered.at[0, pl.ds(q * seg + part_rows, MASK_ROWS)], masks.at[q], mask_sems.at[q]
+        )
+        for q in range(16)
+    ]
+    for copy in copies:
+        copy.start()
     near = parts_of(near_cotangent[...])
     far = parts_of(far_cotangent[...])
     near_t = parts_of(near_cotangent[...].T)
     far_t = parts_of(far_cotangent[...].T)
+    share_rows = out_share // 16
+    near_columns = columns(share * half, half)
     feat_parts[...] = jnp.zeros_like(feat_parts)
-    share_rows = near_cotangent.shape[0] // 16
-    near_out[...] = jnp.zeros_like(near_out)
-    far_out[...] = jnp.zeros_like(far_out)
-
-    def weight_parts(r):
-        return parts_of(near_weights[r]), parts_of(far_weights[r])
-
-    @pl.loop(0, relations + 1)
-    def _(r):
-        @pl.when(r < relations)
-        def _():
-            mixed[...] = jnp.zeros_like(mixed)
-
-            @pl.loop(0, counts[lax.min(r, relations - 1)])
-            def _(t):
-                start = ranks[r, t] * seg + blocks[r, t] * TILE
-                piece = jnp.concatenate(
-                    [gathered[k, rows(start, TILE), :] for k in range(chunks)], axis=1
-                )
-                there = rows(targets[r, t] * TILE, TILE)
-                mixed[there, :] += exact_product(tiles[r * slots + t], piece, ((1,), (0,)))
-
-        own_start = own_rank[0] * seg
-
-        @pl.when(r == relations)
-        def _():
-            for k in range(chunks):
-                mixed[:, k * LANES : (k + 1) * LANES] = gathered[k, rows(own_start, part_rows), :]
-
-        near_w, far_w = weight_parts(r)
-        z = parts_of(mixed[...])
-        near_out[...] += product(near_w, z, ((1,), (1,)))
-        far_out[...] += product(far_w, z, ((1,), (1,)))
+    for copy in copies:
+        copy.wait()
+
+    def feat_start(k, sender):
+        return (rank_of(sender) if k == 0 else other_rank_of(sender)) * part_rows
+
+    def project(r, z, near_w):
+        far_w = parts_of(far_weights[r])
+        near_part = product(near_w, z, ((1,), (1,)))
+        far_part = product(far_w, z, ((1,), (1,)))
         for which, grad in enumerate((near, far)):
             result = product(grad, z, ((1,), (0,)))
             for q in range(16):
+                start = (q * 2 + which) * (relations + 1) * share_rows + r * share_rows
                 for k in range(chunks):
-                    rel_parts[
-                        k, rows(q * 2 * 6 * share_rows + which * 6 * share_rows + r * share_rows, share_rows), :
-                    ] = result[q * share_rows : (q + 1) * share_rows, k * LANES : (k + 1) * LANES]
-        mixed_grad[...] = product(near_t, near_w, ((1,), (0,))) + product(
-            far_t, far_w, ((1,), (0,))
-        )
-
-        @pl.when(r < relations)
-        def _():
-            @pl.loop(0, counts[lax.min(r, relations - 1)])
-            def _(t):
-                start = ranks[r, t] * part_rows + blocks[r, t] * TILE
-                there = rows(targets[r, t] * TILE, TILE)
-                back = exact_product(tiles[r * slots + t], mixed_grad[there, :], ((0,), (0,)))
-                for k in range(chunks):
-                    feat_parts[k, rows(start, TILE), :] += back[:, k * LANES : (k + 1) * LANES]
-
-        @pl.when(r == relations)
-        def _():
+                    rel_parts[k, rows(start, share_rows), :] = result[
+                        q * share_rows : (q + 1) * share_rows, k * LANES : (k + 1) * LANES
+                    ]
+        grad = product(near_t, near_w, ((1,), (0,))) + product(far_t, far_w, ((1,), (0,)))
+        return near_part, far_part, grad
+
+    own = jnp.concatenate(
+        [gathered[k, rows(rank_of(node) * seg, part_rows), :] for k in range(chunks)], axis=1
+    )
+    near_part, far_part, grad = project(
+        relations, parts_of(own), parts_of(self_weight[:, near_columns])
+    )
+    near_out[...] = near_part
+    far_out[...] = far_part
+    for k in range(chunks):
+        feat_parts[k, rows(feat_start(k, node), part_rows), :] = grad[
+            :, k * LANES : (k + 1) * LANES
+        ]
+
+    @pl.loop(0, relations)
+    def _(r):
+        pieces, dense, places = [], [], []
+        for t in range(slots):
+            peer, slot, target = peers[r, t], slot_ids[r, t], targets[r, t]
+            rank = rank_of(peer)
+            at = node * (relations * blocks) + r * blocks
+
+            def marked(b):
+                return masks[rank, lax.div(at + b, LANES), lax.rem(at + b, LANES)] > 0.5
+
+            block = jnp.where(
+                marked(0), jnp.where(marked(1), slot, jnp.int32(0)), jnp.int32(1)
+            )
+            start = rank * seg + block * TILE
+            pieces.append(
+                jnp.concatenate(
+                    [gathered[k, rows(start, TILE), :] for k in range(chunks)], axis=1
+                )
+            )
+            tile = tiles[r * slots + t]
+            alive = t < counts[r]
+            dense.append(
+                jnp.concatenate(
+                    [
+                        tile * jnp.where(alive & (target == b), 1.0, 0.0).astype(tile.dtype)
+                        for b in range(blocks)
+                    ],
+                    axis=0,
+                )
+            )
+            places.append((peer, block))
+        dense = jnp.concatenate(dense, axis=1)
+        z = parts_of(exact_product(dense, jnp.concatenate(pieces, axis=0), ((1,), (0,))))
+        near_part, far_part, grad = project(r, z, parts_of(rel_weights[r, :, near_columns]))
+        near_out[...] += near_part
+        far_out[...] += far_part
+        back = exact_product(dense, grad, ((0,), (0,)))
+        for t, (peer, block) in enumerate(places):
             for k in range(chunks):
-                feat_parts[k, rows(own_rank[0] * part_rows, part_rows), :] += mixed_grad[
-                    :, k * LANES : (k + 1) * LANES
+                feat_parts[k, rows(feat_start(k, peer) + block * TILE, TILE), :] += back[
+                    t * TILE : (t + 1) * TILE, k * LANES : (k + 1) * LANES
                 ]
 
 
@@ -362,15 +420,18 @@
 
 def reduce_kernel(
     feat_parts, rel_parts, far_out, rel_total, feat_total, got_out,
-    feat_sums, rel_sums, send_sems, recv_sems, own_sems,
+    feat_sums, rel_sums, crossed, send_sems, recv_sems, own_sems,
 ):
-    rank, bits, share, partners, across = place()
+    plane_rank, bits, share, plane_partners, across = place()
+    other_rank = bits[0] + 2 * bits[2] + 4 * bits[1] + 8 * bits[3]
+    other_partners = [plane_partners[step] for step in (0, 2, 1, 3)]
     chunks = feat_parts.shape[0]
     feat_seg = feat_parts.shape[1] // 16
     rel_seg = rel_parts.shape[1] // 16
     own_rows = feat_seg // 2
     part = rel_seg // 2
-    greet(partners + [across])
+    relations = rel_total.shape[0]
+    greet(plane_partners + [across])
     sender = Sender(send_sems, recv_sems)
     out_copy = sender.start(far_out, got_out, across)
     local_copies = []
@@ -379,6 +440,9 @@
         inputs, sums, seg = (
             (rel_parts, rel_sums, rel_seg) if kind == "rel" else (feat_parts, feat_sums, feat_seg)
         )
+        swapped = kind == "feat" and k > 0
+        rank = other_rank if swapped else plane_rank
+        partners = other_partners if swapped else plane_partners
         copy = None
         for step in (3, 2, 1, 0, -1):
             if copy is not None:
@@ -409,55 +473,60 @@
                 source, sums.at[k, rows((size - 1) * seg, size * seg)], partners[step]
             )
             yield
-        where = share * chunks + k
+        where = columns((share * chunks + k) * LANES, LANES)
         if kind == "feat":
             cross = sender.start(
-                sums.at[k, rows((1 - share) * own_rows, own_rows)], feat_total.at[where], across
+                sums.at[k, rows((1 - share) * own_rows, own_rows)],
+                feat_total.at[:, where],
+                across,
             )
             local = pltpu.make_async_copy(
-                sums.at[k, rows(share * own_rows, own_rows)],
-                feat_total.at[where],
-                own_sems.at[chunks + k],
+                sums.at[k, rows(share * own_rows, own_rows)], feat_total.at[:, where],
+                own_sems.at[k],
             )
             local.start()
             local_copies.append(local)
             yield
             cross.wait_recv()
             return
-        cross = sender.start(
-            sums.at[k, pl.ds(part, part)], rel_total.at[where, rows(rank * part, part)], across
-        )
-        local = pltpu.make_async_copy(
-            sums.at[k, pl.ds(0, part)],
-            rel_total.at[where, rows(rank * part, part)],
-            own_sems.at[k],
-        )
-        local.start()
-        local.wait()
-        waiting = [None, cross]
+        cross = sender.start(sums.at[k, pl.ds(part, part)], crossed.at[k], across)
+        own_share = part // relations
+        own_place = rows(rank * own_share, own_share)
+        for r in range(relations):
+            rel_total[r, own_place, where] = sums[k, r * own_share : (r + 1) * own_share, :]
+        waiting = [None, None]
         for wave in range(STEPS + 2):
             for piece in range(2):
                 step = wave - piece
                 if step < 0 or step > STEPS:
                     continue
+                spot = share if piece == 0 else 1 - share
+                there = columns((spot * chunks + k) * LANES, LANES)
                 if waiting[piece] is not None:
                     waiting[piece].wait_recv()
+                elif piece == 1:
+                    cross.wait_recv()
+                    for r in range(relations):
+                        rel_total[r, own_place, there] = crossed[
+                            k, r * own_share : (r + 1) * own_share, :
+                        ]
                 if step == STEPS:
                     continue
-                size = 1 << step
-                index = (share if piece == 0 else 1 - share) * chunks + k
+                size = (1 << step) * own_share
                 held = rel_total.at[
-                    index, rows(lax.div(rank, jnp.int32(size)) * (size * part), size * part)
+                    :, rows(lax.div(rank, jnp.int32(1 << step)) * size, size), there
                 ]
                 waiting[piece] = sender.start(held, held, partners[step])
             yield
 
     chains = [chain("rel", k) for k in range(chunks)] + [chain("feat", k) for k in range(chunks)]
+    for one in chains:
+        next(one)
     active = []
     while chains or active:
         if chains:
             active.append(chains.pop(0))
-        for one in list(active):
+        for one in reversed(list(active)):
             if next(one, "end") == "end":
                 active.remove(one)
     out_copy.wait_recv()
@@ -478,7 +547,6 @@
     relations, out_share, features = rel_weights.shape
     part_rows = cotangent.shape[1]
     own_rows = node_feats.shape[0]
-    blocks = part_rows // TILE
     parts = lax.axis_size("nodes")
     half = features // 2
     chunks = half // LANES
@@ -499,8 +567,8 @@
         in_specs=vmem(5),
         out_specs=tuple(vmem(3)),
         scratch_shapes=[
-            pltpu.SemaphoreType.DMA((32,)),
-            pltpu.SemaphoreType.DMA((32,)),
+            pltpu.SemaphoreType.DMA((40,)),
+            pltpu.SemaphoreType.DMA((40,)),
             pltpu.SemaphoreType.DMA((2 * chunks,)),
         ],
         compiler_params=pltpu.CompilerParams(
@@ -508,26 +576,7 @@
         ),
         name="gather_nodes",
     )(node_feats, rel_weights, self_weight, cotangent, mask)
-    masks = gathered[0].reshape(parts, seg, LANES)[:, part_rows:].reshape(parts, -1)
-    columns_all = relations * blocks
-    masks = masks[:, : parts * columns_all].reshape(parts, parts, columns_all)
-    to_me = jnp.sum(
-        masks * (jnp.arange(parts) == node).astype(f32)[None, :, None], axis=1
-    ).astype(jnp.int32)
-    peer = tile_peer[0]
-    peer_rank = rank_of(peer)
-    picked = jnp.sum(
-        jnp.where(peer_rank[:, :, None, None] == jnp.arange(parts)[None, None, :, None], to_me, 0),
-        axis=2,
-    )
-    order = jnp.cumsum(picked, axis=2) - 1
-    found = (picked == 1) & (order == tile_slot[0][:, :, None])
-    column = jnp.sum(jnp.where(found, jnp.arange(columns_all)[None, None, :], 0), axis=2)
-    block = (column % blocks).astype(jnp.int32)
-    near_weights = lax.dynamic_slice_in_dim(
-        jnp.concatenate([rel_weights, self_weight[None]]), share * half, half, 2
-    )
-    own_rank = rank_of(node).astype(jnp.int32).reshape(1)
+    me = jnp.stack([node, share]).astype(jnp.int32)
     rel_rows = (relations + 1) * out_share // parts
     smem = [pl.BlockSpec(memory_space=pltpu.SMEM)] * 5
     near_out, far_out, feat_parts, rel_parts = pl.pallas_call(
@@ -538,21 +587,24 @@
             shape((chunks, parts * part_rows, LANES), f32),
             shape((chunks, parts * 2 * rel_rows, LANES), f32),
         ),
-        in_specs=smem + vmem(6),
+        in_specs=smem + vmem(7),
         out_specs=tuple(vmem(4)),
-        scratch_shapes=[pltpu.VMEM((part_rows, half), f32), pltpu.VMEM((part_rows, half), f32)],
+        scratch_shapes=[
+            pltpu.SMEM((parts, MASK_ROWS, LANES), f32),
+            pltpu.SemaphoreType.DMA((parts,)),
+        ],
         compiler_params=pltpu.CompilerParams(vmem_limit_bytes=VMEM_LIMIT),
         name="local_products",
     )(
-        tile_count[0], peer_rank, block, tile_target[0], own_rank,
+        tile_count[0], tile_peer[0], tile_slot[0], tile_target[0], me,
         tile_values[0].reshape(relations * slots, TILE, TILE),
-        gathered, near_weights, far_weights, cotangent, far_cotangent,
+        gathered, rel_weights, self_weight, far_weights, cotangent, far_cotangent,
     )
     rel_total, feat_total, got_out = pl.pallas_call(
         reduce_kernel,
         out_shape=(
-            shape((2 * chunks, parts * rel_rows, LANES), f32),
-            shape((2 * chunks, own_rows, LANES), f32),
+            shape((relations + 1, out_share, features), f32),
+            shape((own_rows, features), f32),
             shape((out_share, part_rows), f32),
         ),
         in_specs=vmem(3),
@@ -560,6 +612,7 @@
         scratch_shapes=[
             pltpu.VMEM((chunks, 15 * part_rows, LANES), f32),
             pltpu.VMEM((chunks, 15 * 2 * rel_rows, LANES), f32),
+            pltpu.VMEM((chunks, rel_rows, LANES), f32),
             pltpu.SemaphoreType.DMA((72,)),
             pltpu.SemaphoreType.DMA((72,)),
             pltpu.SemaphoreType.DMA((2 * chunks,)),
@@ -570,11 +623,8 @@
         name="reduce_grads",
     )(feat_parts, rel_parts, far_out)
     layer_out = near_out + got_out
-    feat_grad = feat_total.transpose(1, 0, 2).reshape(own_rows, features)
     factor = float(part_rows * parts) ** (-0.5)
-    totals = rel_total.reshape(2 * chunks, parts, relations + 1, out_share // parts, LANES)
-    totals = totals.transpose(2, 1, 3, 0, 4).reshape(relations + 1, out_share, features) * factor
-    return (layer_out, feat_grad, totals[:relations], totals[relations])
+    return (layer_out, feat_total, rel_total[:relations] * factor, rel_total[relations] * factor)
 
 
 def local(node_feats, rel_weights, self_weight, cotangent, *tiles):

time: 237 us -> 219 us (0.924)
  local copies, waits for them, and re-layouts: 19.5 us -> 4.1 us
    pallas_call x1, Pallas kernels: 106 us -> 121 us  [plane_gather(): pl.pallas_call(reduce_kernel, out_shape=(shape((relations + 1, out_share,...]
    pallas_call x1, Pallas kernels: 69.9 us -> 58 us  [plane_gather(): pl.pallas_call(gather_kernel, out_shape=(shape((chunks, parts * seg, LANE...]
    slice x6 -> x0, local copies, waits for them, and re-layouts: 10.6 us -> none  [the longest x3 8.83 us: plane_gather(): return (layer_out, feat_grad, totals[:relations], totals[relations])]
    pallas_call x1, Pallas kernels: 29.8 us -> 25.2 us  [plane_gather(): pl.pallas_call(compute_kernel, out_shape=(shape((out_share, part_rows), f...]
    mul x1 -> x2, other arithmetic: 2.64 us -> 6.57 us  [the longest x1 4.45 us: plane_gather(): rel_total[:relations] * factor]
    concatenate x1 -> x0, other arithmetic: 3.14 us -> none  [plane_gather(): jnp.concatenate([rel_weights, self_weight[None]])]
    mul x1 -> x0, local copies, waits for them, and re-layouts: 2.83 us -> none  [plane_gather(): totals.transpose(2, 1, 3, 0, 4).reshape(relations + 1, out_share, features)]
where the time goes in v1:
time: 219 us; the launch traced here: 218 us
  Pallas kernels  204 us (93%)
  other arithmetic  9.62 us (4%)
  local copies, waits for them, and re-layouts  4.1 us (2%)
    pallas_call x1, Pallas kernels, plane_gather(): pl.pallas_call(reduce_kernel, out_shape=(shape((relations + 1, out_share,...  121 us
    pallas_call x1, Pallas kernels, plane_gather(): pl.pallas_call(gather_kernel, out_shape=(shape((chunks, parts * seg, LANE...  58 us
    pallas_call x1, Pallas kernels, plane_gather(): pl.pallas_call(compute_kernel, out_shape=(shape((out_share, part_rows), f...  25.2 us
    mul x1, other arithmetic, plane_gather(): rel_total[:relations] * factor  4.45 us

profile of v1, /device:TPU:1, one launch (start us, length us, event | category | flops | bytes accessed | tf_op | source)
XLA Modules:
  0.0 218.4 jit_solution(17500067753527155955)
XLA Ops:
  0.6 0.7 pad_add_fusion.me
  1.3 1.3 copy.21
  2.6 0.7 convert_element_type.9
  3.3 0.1 copy.14
  3.4 0.1 convert_element_type.10
  3.4 0.6 pad_bitcast_fusion.mask
  4.0 1.3 copy_bitcast_fusion
  5.3 58.0 %gather_nodes.1 = (f32[3,4224,128]{2,1,0:T(8,128)}, f32[6,256,384]{2,1,0:T(8,128)}, f32[256,256]{1,0:T(8,128)}) custom-call(f32[128,768]{1,0:T(8,128)} %feats.1, f32[5,256,768]{2,1,0:T(8,128)} %rel_weights.3, f32[256,768]{1,0:T(8,128)} %self_weight.3, f32[256,256]{1,0:T(8,128)} %near_cotangent.1, f32[8,128]{1,0:T(8,128)} %pad_bitcast_fusion.mask), custom_call_target="tpu_custom_call" | custom-call | tf_op jit(solution)/shard_map/gather_nodes/pallas_call | solution.py:560
  63.3 25.2 %local_products.1 = (f32[256,256]{1,0:T(8,128)}, f32[256,256]{1,0:T(8,128)}, f32[3,4096,128]{2,1,0:T(8,128)}, f32[3,3072,128]{2,1,0:T(8,128)}) custom-call(s32[5]{0:T(128)} %bitcast.17, s32[5,6]{1,0:T(8,128)} %bitcast.16, s32[5,6]{1,0:T(8,128)} %get-tuple-element.25.slot_ids, s32[5,6]{1,0:T(8,128)} %get-tuple-element.24.targets, s32[2]{0:T(128)} %pad_add_fusion.me, ...), custom_call_target="tpu_custom_call" | custom-call | tf_op jit(solution)/shard_map/local_products/pallas_call | solution.py:582
  88.5 0.0 copy-start.1
  88.5 120.8 %reduce_grads.1 = (f32[6,256,768]{2,1,0:T(8,128)}, f32[128,768]{1,0:T(8,128)}, f32[256,256]{1,0:T(8,128)}) custom-call(f32[3,4096,128]{2,1,0:T(8,128)} %get-tuple-element.18.feat_parts, f32[3,3072,128]{2,1,0:T(8,128)} %get-tuple-element.19.rel_parts, f32[256,256]{1,0:T(8,128)} %get-tuple-element.20.far_out), custom_call_target="tpu_custom_call" | custom-call | tf_op jit(solution)/shard_map/reduce_grads/pallas_call | solution.py:603
  209.4 0.0 copy-done.1
  209.4 1.7 add.5
  211.1 0.0 copy-start
  211.1 2.1 multiply_bitcast_fusion
  213.2 4.5 %slice_multiply_fusion = f32[5,256,768]{2,1,0:T(8,128)} fusion(f32[6,256,768]{2,1,0:T(8,128)} %get-tuple-element.23), kind=kLoop, calls=%fused_computation | loop fusion | flops 983040 | bytes 7864320 | tf_op jit(solution)/shard_map/mul | solution.py:627
  217.7 0.0 copy-done
  217.7 0.7 copy.23
Async XLA Ops:
  88.5 120.9 %copy-start.1 = (f32[256,256]{1,0:T(8,128)S(1)}, f32[256,256]{1,0:T(8,128)}, u32[]{:S(2)}) copy-start(f32[256,256]{1,0:T(8,128)} %get-tuple-element.17) | copy-start | bytes 786436
  211.1 6.6 %copy-start = (f32[128,768]{1,0:T(8,128)S(1)}, f32[128,768]{1,0:T(8,128)}, u32[]{:S(2)}) copy-start(f32[128,768]{1,0:T(8,128)} %get-tuple-element.31) | copy-start | bytes 1179652

commit v2 on v1

--- a/solution.py
+++ b/solution.py
@@ -123,11 +123,6 @@
 def rank_of(node):
     z1, z0, y, core = (bit_of(node, weight) for weight in (8, 4, 2, 1))
     return z1 + 2 * z0 + 4 * y + 8 * core
-
-
-def other_rank_of(node):
-    z1, z0, y, core = (bit_of(node, weight) for weight in (8, 4, 2, 1))
-    return z1 + 2 * y + 4 * z0 + 8 * core
 
 
 def greet(devices):
@@ -303,10 +298,10 @@
 
 
 def compute_kernel(
-    counts, peers, slot_ids, targets, me, tiles, gathered, rel_weights, self_weight, far_weights,
+    codes, me, tiles, gathered, rel_weights, self_weight, far_weights,
     near_cotangent, far_cotangent, near_out, far_out, feat_parts, rel_parts, masks, mask_sems,
 ):
-    relations, slots = peers.shape
+    relations, slots = codes.shape
     chunks = gathered.shape[0]
     half = chunks * LANES
     out_share, part_rows = near_cotangent.shape
@@ -331,8 +326,8 @@
     for copy in copies:
         copy.wait()
 
-    def feat_start(k, sender):
-        return (rank_of(sender) if k == 0 else other_rank_of(sender)) * part_rows
+    def feat_start(sender):
+        return rank_of(sender) * part_rows
 
     def project(r, z, near_w):
         far_w = parts_of(far_weights[r])
@@ -358,7 +353,7 @@
     near_out[...] = near_part
     far_out[...] = far_part
     for k in range(chunks):
-        feat_parts[k, rows(feat_start(k, node), part_rows), :] = grad[
+        feat_parts[k, rows(feat_start(node), part_rows), :] = grad[
             :, k * LANES : (k + 1) * LANES
         ]
 
@@ -366,7 +361,9 @@
     def _(r):
         pieces, dense, places = [], [], []
         for t in range(slots):
-            peer, slot, target = peers[r, t], slot_ids[r, t], targets[r, t]
+            code = codes[r, t]
+            alive, target, slot = (bit_of(code, weight) == 1 for weight in (1, 2, 4))
+            peer = lax.div(code, jnp.int32(8))
             rank = rank_of(peer)
             at = node * (relations * blocks) + r * blocks
 
@@ -374,7 +371,7 @@
                 return masks[rank, lax.div(at + b, LANES), lax.rem(at + b, LANES)] > 0.5
 
             block = jnp.where(
-                marked(0), jnp.where(marked(1), slot, jnp.int32(0)), jnp.int32(1)
+                marked(0), jnp.where(marked(1) & slot, jnp.int32(1), jnp.int32(0)), jnp.int32(1)
             )
             start = rank * seg + block * TILE
             pieces.append(
@@ -383,11 +380,10 @@
                 )
             )
             tile = tiles[r * slots + t]
-            alive = t < counts[r]
             dense.append(
                 jnp.concatenate(
                     [
-                        tile * jnp.where(alive & (target == b), 1.0, 0.0).astype(tile.dtype)
+                        tile * jnp.where(alive & (target if b == 1 else ~target), 1.0, 0.0).astype(tile.dtype)
                         for b in range(blocks)
                     ],
                     axis=0,
@@ -402,13 +398,12 @@
         back = exact_product(dense, grad, ((0,), (0,)))
         for t, (peer, block) in enumerate(places):
             for k in range(chunks):
-                feat_parts[k, rows(feat_start(k, peer) + block * TILE, TILE), :] += back[
+                feat_parts[k, rows(feat_start(peer) + block * TILE, TILE), :] += back[
                     t * TILE : (t + 1) * TILE, k * LANES : (k + 1) * LANES
                 ]
 
 
-def add_rows(target, target_start, source, source_start, count):
-    block = 64
+def add_rows(target, target_start, source, source_start, count, block):
 
     def body(i, carry):
         there = rows(target_start + i * block, block)
@@ -419,19 +414,17 @@
 
 
 def reduce_kernel(
-    feat_parts, rel_parts, far_out, rel_total, feat_total, got_out,
+    feat_parts, rel_parts, far_out, rel_total, self_total, feat_total, got_out,
     feat_sums, rel_sums, crossed, send_sems, recv_sems, own_sems,
 ):
-    plane_rank, bits, share, plane_partners, across = place()
-    other_rank = bits[0] + 2 * bits[2] + 4 * bits[1] + 8 * bits[3]
-    other_partners = [plane_partners[step] for step in (0, 2, 1, 3)]
+    rank, bits, share, partners, across = place()
     chunks = feat_parts.shape[0]
     feat_seg = feat_parts.shape[1] // 16
     rel_seg = rel_parts.shape[1] // 16
     own_rows = feat_seg // 2
     part = rel_seg // 2
     relations = rel_total.shape[0]
-    greet(plane_partners + [across])
+    greet(partners + [across])
     sender = Sender(send_sems, recv_sems)
     out_copy = sender.start(far_out, got_out, across)
     local_copies = []
@@ -440,9 +433,6 @@
         inputs, sums, seg = (
             (rel_parts, rel_sums, rel_seg) if kind == "rel" else (feat_parts, feat_sums, feat_seg)
         )
-        swapped = kind == "feat" and k > 0
-        rank = other_rank if swapped else plane_rank
-        partners = other_partners if swapped else plane_partners
         copy = None
         for step in (3, 2, 1, 0, -1):
             if copy is not None:
@@ -452,12 +442,12 @@
                 if step == 2:
                     add_rows(
                         sums.at[k], (size - 1) * seg, inputs.at[k],
-                        lax.div(rank, jnp.int32(8)) * (8 * seg), size * seg,
+                        lax.div(rank, jnp.int32(8)) * (8 * seg), size * seg, seg,
                     )
                 else:
                     add_rows(
                         sums.at[k], (size - 1) * seg, sums.at[k],
-                        (2 * size - 1) * seg + mine, size * seg,
+                        (2 * size - 1) * seg + mine, size * seg, seg,
                     )
             if step < 0:
                 break
@@ -490,11 +480,12 @@
             cross.wait_recv()
             return
         cross = sender.start(sums.at[k, pl.ds(part, part)], crossed.at[k], across)
-        own_share = part // relations
+        own_share = part // (relations + 1)
         own_place = rows(rank * own_share, own_share)
         for r in range(relations):
             rel_total[r, own_place, where] = sums[k, r * own_share : (r + 1) * own_share, :]
-        waiting = [None, None]
+        self_total[own_place, where] = sums[k, relations * own_share : part, :]
+        waiting = [(), ()]
         for wave in range(STEPS + 2):
             for piece in range(2):
                 step = wave - piece
@@ -502,28 +493,31 @@
                     continue
                 spot = share if piece == 0 else 1 - share
                 there = columns((spot * chunks + k) * LANES, LANES)
-                if waiting[piece] is not None:
-                    waiting[piece].wait_recv()
-                elif piece == 1:
+                for copy in waiting[piece]:
+                    copy.wait_recv()
+                if piece == 1 and step == 0:
                     cross.wait_recv()
                     for r in range(relations):
                         rel_total[r, own_place, there] = crossed[
                             k, r * own_share : (r + 1) * own_share, :
                         ]
+                    self_total[own_place, there] = crossed[k, relations * own_share : part, :]
                 if step == STEPS:
                     continue
                 size = (1 << step) * own_share
-                held = rel_total.at[
-                    :, rows(lax.div(rank, jnp.int32(1 << step)) * size, size), there
+                span = rows(lax.div(rank, jnp.int32(1 << step)) * size, size)
+                waiting[piece] = [
+                    sender.start(held, held, partners[step])
+                    for held in (rel_total.at[:, span, there], self_total.at[span, there])
                 ]
-                waiting[piece] = sender.start(held, held, partners[step])
             yield
 
     chains = [chain("rel", k) for k in range(chunks)] + [chain("feat", k) for k in range(chunks)]
-    for one in chains:
-        next(one)
+    next(chains[0])
     active = []
     while chains or active:
+        if len(chains) > 1:
+            next(chains[1])
         if chains:
             active.append(chains.pop(0))
         for one in reversed(list(active)):
@@ -576,9 +570,11 @@
         ),
         name="gather_nodes",
     )(node_feats, rel_weights, self_weight, cotangent, mask)
+    alive = jnp.arange(slots, dtype=jnp.int32)[None, :] < tile_count[0][:, None]
+    codes = tile_peer[0] * 8 + tile_slot[0] * 4 + tile_target[0] * 2 + alive.astype(jnp.int32)
     me = jnp.stack([node, share]).astype(jnp.int32)
     rel_rows = (relations + 1) * out_share // parts
-    smem = [pl.BlockSpec(memory_space=pltpu.SMEM)] * 5
+    smem = [pl.BlockSpec(memory_space=pltpu.SMEM)] * 2
     near_out, far_out, feat_parts, rel_parts = pl.pallas_call(
         compute_kernel,
         out_shape=(
@@ -596,25 +592,26 @@
         compiler_params=pltpu.CompilerParams(vmem_limit_bytes=VMEM_LIMIT),
         name="local_products",
     )(
-        tile_count[0], tile_peer[0], tile_slot[0], tile_target[0], me,
+        codes, me,
         tile_values[0].reshape(relations * slots, TILE, TILE),
         gathered, rel_weights, self_weight, far_weights, cotangent, far_cotangent,
     )
-    rel_total, feat_total, got_out = pl.pallas_call(
+    rel_total, self_total, feat_total, got_out = pl.pallas_call(
         reduce_kernel,
         out_shape=(
-            shape((relations + 1, out_share, features), f32),
+            shape((relations, out_share, features), f32),
+            shape((out_share, features), f32),
             shape((own_rows, features), f32),
             shape((out_share, part_rows), f32),
         ),
         in_specs=vmem(3),
-        out_specs=tuple(vmem(3)),
+        out_specs=tuple(vmem(4)),
         scratch_shapes=[
             pltpu.VMEM((chunks, 15 * part_rows, LANES), f32),
             pltpu.VMEM((chunks, 15 * 2 * rel_rows, LANES), f32),
             pltpu.VMEM((chunks, rel_rows, LANES), f32),
-            pltpu.SemaphoreType.DMA((72,)),
-            pltpu.SemaphoreType.DMA((72,)),
+            pltpu.SemaphoreType.DMA((96,)),
+            pltpu.SemaphoreType.DMA((96,)),
             pltpu.SemaphoreType.DMA((2 * chunks,)),
         ],
         compiler_params=pltpu.CompilerParams(
@@ -624,7 +621,7 @@
     )(feat_parts, rel_parts, far_out)
     layer_out = near_out + got_out
     factor = float(part_rows * parts) ** (-0.5)
-    return (layer_out, feat_total, rel_total[:relations] * factor, rel_total[relations] * factor)
+    return (layer_out, feat_total, rel_total * factor, self_total * factor)
 
 
 def local(node_feats, rel_weights, self_weight, cotangent, *tiles):

time: 219 us -> 206 us (0.941)
  Pallas kernels: 204 us -> 193 us
  local copies, waits for them, and re-layouts: 4.1 us -> 1.53 us
    pallas_call x1, Pallas kernels: 121 us -> 109 us  [plane_gather(): pl.pallas_call(reduce_kernel, out_shape=(shape((relations, out_share, fea...]
    unnamed x7 -> x5, local copies, waits for them, and re-layouts: 3.33 us -> 0.76 us
where the time goes in v2:
time: 206 us
  Pallas kernels  193 us (94%)
  other arithmetic  10.9 us (5%)
    pallas_call x1, Pallas kernels, plane_gather(): pl.pallas_call(reduce_kernel, out_shape=(shape((relations, out_share, fea...  109 us
    pallas_call x1, Pallas kernels, plane_gather(): pl.pallas_call(gather_kernel, out_shape=(shape((chunks, parts * seg, LANE...  58 us
    pallas_call x1, Pallas kernels, plane_gather(): pl.pallas_call(compute_kernel, out_shape=(shape((out_share, part_rows), f...  25.6 us
    mul x2, other arithmetic, plane_gather(): return (layer_out, feat_total, rel_total * factor, self_total * factor)  6.57 us

profile of v2, /device:TPU:1, one launch (start us, length us, event | category | flops | bytes accessed | tf_op | source)
XLA Modules:
  0.0 206.0 jit_solution(7214143546785999857)
XLA Ops:
  0.6 0.6 pad_add_fusion.me
  1.2 1.4 bitcast_add_fusion.codes
  2.6 0.7 convert_element_type.13
  3.3 0.1 copy.20
  3.4 0.1 convert_element_type.14
  3.5 0.6 pad_bitcast_fusion.mask
  4.1 58.0 %gather_nodes.1 = (f32[3,4224,128]{2,1,0:T(8,128)}, f32[6,256,384]{2,1,0:T(8,128)}, f32[256,256]{1,0:T(8,128)}) custom-call(f32[128,768]{1,0:T(8,128)} %feats.1, f32[5,256,768]{2,1,0:T(8,128)} %rel_weights.3, f32[256,768]{1,0:T(8,128)} %self_weight.3, f32[256,256]{1,0:T(8,128)} %near_cotangent.1, f32[8,128]{1,0:T(8,128)} %pad_bitcast_fusion.mask), custom_call_target="tpu_custom_call" | custom-call | tf_op jit(solution)/shard_map/gather_nodes/pallas_call | solution.py:554
  62.1 25.6 %local_products.1 = (f32[256,256]{1,0:T(8,128)}, f32[256,256]{1,0:T(8,128)}, f32[3,4096,128]{2,1,0:T(8,128)}, f32[3,3072,128]{2,1,0:T(8,128)}) custom-call(s32[5,6]{1,0:T(8,128)} %bitcast_add_fusion.codes, s32[2]{0:T(128)} %pad_add_fusion.me, bf16[30,128,128]{2,1,0:T(8,128)(2,1)} %bitcast.8, f32[3,4224,128]{2,1,0:T(8,128)} %get-tuple-element.15.gathered, ...), custom_call_target="tpu_custom_call" | custom-call | tf_op jit(solution)/shard_map/local_products/pallas_call | solution.py:578
  87.6 0.0 copy-start.1
  87.7 109.3 %reduce_grads.1 = (f32[5,256,768]{2,1,0:T(8,128)}, f32[256,768]{1,0:T(8,128)}, f32[128,768]{1,0:T(8,128)}, f32[256,256]{1,0:T(8,128)}) custom-call(f32[3,4096,128]{2,1,0:T(8,128)} %get-tuple-element.19.feat_parts, f32[3,3072,128]{2,1,0:T(8,128)} %get-tuple-element.20.rel_parts, f32[256,256]{1,0:T(8,128)} %get-tuple-element.21.far_out), custom_call_target="tpu_custom_call" | custom-call | tf_op jit(solution)/shard_map/reduce_grads/pallas_call | solution.py:599
  197.0 0.0 copy-done.1
  197.0 1.7 add.22
  198.7 2.1 %broadcast_multiply_fusion.1 = f32[256,768]{1,0:T(8,128)} fusion(f32[256,768]{1,0:T(8,128)} %get-tuple-element.25), kind=kLoop, calls=%fused_computation.1 | loop fusion | flops 196608 | bytes 1572864 | tf_op jit(solution)/shard_map/mul | solution.py:624
  200.8 0.0 copy-start
  200.8 4.5 %broadcast_multiply_fusion = f32[5,256,768]{2,1,0:T(8,128)} fusion(f32[5,256,768]{2,1,0:T(8,128)} %get-tuple-element.24), kind=kLoop, calls=%fused_computation | loop fusion | flops 983040 | bytes 7864320 | tf_op jit(solution)/shard_map/mul | solution.py:624
  205.3 0.0 copy-done
  205.3 0.7 copy.35
Async XLA Ops:
  87.6 109.3 %copy-start.1 = (f32[256,256]{1,0:T(8,128)S(1)}, f32[256,256]{1,0:T(8,128)}, u32[]{:S(2)}) copy-start(f32[256,256]{1,0:T(8,128)} %get-tuple-element.18) | copy-start | bytes 786436
  200.8 4.5 %copy-start = (f32[128,768]{1,0:T(8,128)S(1)}, f32[128,768]{1,0:T(8,128)}, u32[]{:S(2)}) copy-start(f32[128,768]{1,0:T(8,128)} %get-tuple-element.31) | copy-start | bytes 1179652

commit v3 on v2

--- a/solution.py
+++ b/solution.py
@@ -99,7 +99,7 @@
 
 LANES = 128
 MASK_ROWS = 8
-VMEM_LIMIT = 60 * 1024 * 1024
+MIB = 1024 * 1024
 MESH = pl.DeviceIdType.MESH
 STEPS = 4
 
@@ -566,7 +566,7 @@
             pltpu.SemaphoreType.DMA((2 * chunks,)),
         ],
         compiler_params=pltpu.CompilerParams(
-            collective_id=0, has_side_effects=True, vmem_limit_bytes=VMEM_LIMIT
+            collective_id=0, has_side_effects=True, vmem_limit_bytes=16 * MIB
         ),
         name="gather_nodes",
     )(node_feats, rel_weights, self_weight, cotangent, mask)
@@ -589,7 +589,7 @@
             pltpu.SMEM((parts, MASK_ROWS, LANES), f32),
             pltpu.SemaphoreType.DMA((parts,)),
         ],
-        compiler_params=pltpu.CompilerParams(vmem_limit_bytes=VMEM_LIMIT),
+        compiler_params=pltpu.CompilerParams(vmem_limit_bytes=28 * MIB),
         name="local_products",
     )(
         codes, me,
@@ -615,7 +615,7 @@
             pltpu.SemaphoreType.DMA((2 * chunks,)),
         ],
         compiler_params=pltpu.CompilerParams(
-            collective_id=1, has_side_effects=True, vmem_limit_bytes=VMEM_LIMIT
+            collective_id=1, has_side_effects=True, vmem_limit_bytes=28 * MIB
         ),
         name="reduce_grads",
     )(feat_parts, rel_parts, far_out)

time: 206 us -> 186 us (0.903)
  Pallas kernels: 193 us -> 172 us
  local copies, waits for them, and re-layouts: 1.53 us -> 7.31 us
  other arithmetic: 10.9 us -> 5.53 us
    pallas_call x1, Pallas kernels: 25.6 us -> 16.9 us  [plane_gather(): pl.pallas_call(compute_kernel, out_shape=(shape((out_share, part_rows), f...]
    unnamed x5 -> x17, local copies, waits for them, and re-layouts: 0.76 us -> 7.14 us
    pallas_call x1, Pallas kernels: 109 us -> 103 us  [plane_gather(): pl.pallas_call(reduce_kernel, out_shape=(shape((relations, out_share, fea...]
    pallas_call x1, Pallas kernels: 58 us -> 51.9 us  [plane_gather(): pl.pallas_call(gather_kernel, out_shape=(shape((chunks, parts * seg, LANE...]
    mul x2, other arithmetic: 6.57 us -> 3.23 us  [plane_gather(): return (layer_out, feat_total, rel_total * factor, self_total * factor)]
where the time goes in v3:
time: 186 us; the launch traced here: 185 us
  Pallas kernels  172 us (92%)
  local copies, waits for them, and re-layouts  7.31 us (4%)
  other arithmetic  5.53 us (3%)
    pallas_call x1, Pallas kernels, plane_gather(): pl.pallas_call(reduce_kernel, out_shape=(shape((relations, out_share, fea...  103 us
    pallas_call x1, Pallas kernels, plane_gather(): pl.pallas_call(gather_kernel, out_shape=(shape((chunks, parts * seg, LANE...  51.9 us
    pallas_call x1, Pallas kernels, plane_gather(): pl.pallas_call(compute_kernel, out_shape=(shape((out_share, part_rows), f...  16.9 us
    unnamed x17, local copies, waits for them, and re-layouts  7.14 us

profile of v3, /device:TPU:1, one launch (start us, length us, event | category | flops | bytes accessed | tf_op | source)
XLA Modules:
  0.0 185.3 jit_solution(12896452137219565987)
XLA Ops:
  0.6 0.1 pad_add_fusion.me
  0.7 0.8 bitcast_add_fusion.codes
  1.5 0.7 convert_element_type.13
  2.2 0.1 copy.20
  2.3 0.1 convert_element_type.14
  2.4 0.0 copy-start
  2.4 2.1 %copy-done = f32[5,256,768]{2,1,0:T(8,128)S(1)} copy-done((f32[5,256,768]{2,1,0:T(8,128)S(1)}, f32[5,256,768]{2,1,0:T(8,128)}, u32[]{:S(2)}) %copy-start) | copy-done | bytes 3932184
  4.5 0.0 copy-start.2
  4.5 1.1 copy-done.2
  5.6 0.0 copy-start.4
  5.6 0.9 copy-done.4
  6.6 0.0 copy-start.7
  6.6 1.0 copy-done.7
  7.6 0.0 copy-start.1
  7.6 0.0 copy-start.3
  7.6 0.0 copy-start.5
  7.6 51.9 %gather_nodes.1 = (f32[3,4224,128]{2,1,0:T(8,128)S(1)}, f32[6,256,384]{2,1,0:T(8,128)S(1)}, f32[256,256]{1,0:T(8,128)S(1)}) custom-call(f32[128,768]{1,0:T(8,128)S(1)} %copy-done.7, f32[5,256,768]{2,1,0:T(8,128)S(1)} %copy-done, f32[256,768]{1,0:T(8,128)S(1)} %copy-done.2, f32[256,256]{1,0:T(8,128)S(1)} %copy-done.4, f32[8,128]{1,0:T(8,128)S(1)} %pad_bitcast_fusion.mask), custom_call_target="tpu_custom_call" | custom-call | tf_op jit(solution)/shard_map/gather_nodes/pallas_call | solution.py:554
  59.5 0.0 copy-done.1
  59.5 0.0 copy-done.3
  59.5 0.0 copy-done.5
  59.5 0.0 copy-start.6
  59.5 1.2 copy-done.6
  60.7 16.9 %local_products.1 = (f32[256,256]{1,0:T(8,128)S(1)}, f32[256,256]{1,0:T(8,128)S(1)}, f32[3,4096,128]{2,1,0:T(8,128)S(1)}, f32[3,3072,128]{2,1,0:T(8,128)S(1)}) custom-call(s32[5,6]{1,0:T(8,128)S(1)} %bitcast_add_fusion.codes, s32[2]{0:T(128)S(1)} %pad_add_fusion.me, bf16[30,128,128]{2,1,0:T(8,128)(2,1)S(1)} %bitcast.8, ...), custom_call_target="tpu_custom_call" | custom-call | tf_op jit(solution)/shard_map/local_products/pallas_call | solution.py:578
  77.6 103.0 %reduce_grads.1 = (f32[5,256,768]{2,1,0:T(8,128)S(1)}, f32[256,768]{1,0:T(8,128)S(1)}, f32[128,768]{1,0:T(8,128)S(1)}, f32[256,256]{1,0:T(8,128)S(1)}) custom-call(f32[3,4096,128]{2,1,0:T(8,128)S(1)} %get-tuple-element.19.feat_parts, f32[3,3072,128]{2,1,0:T(8,128)S(1)} %get-tuple-element.20.rel_parts, f32[256,256]{1,0:T(8,128)S(1)} %get-tuple-element.21.far_out), custom_call_target="tpu_custom_call" | custom-call | tf_op jit(solution)/shard_map/reduce_grads/pallas_call | solution.py:599
  180.6 0.7 add.22
  181.3 0.9 broadcast_multiply_fusion.1
  182.3 2.3 %broadcast_multiply_fusion = f32[5,256,768]{2,1,0:T(8,128)} fusion(f32[5,256,768]{2,1,0:T(8,128)S(1)} %get-tuple-element.24), kind=kLoop, calls=%fused_computation | loop fusion | flops 983040 | bytes 7864320 | tf_op jit(solution)/shard_map/mul | solution.py:624
  184.6 0.7 copy.35
  (1 shorter events, 0.0 us)
Async XLA Ops:
  2.4 2.1 %copy-start = (f32[5,256,768]{2,1,0:T(8,128)S(1)}, f32[5,256,768]{2,1,0:T(8,128)}, u32[]{:S(2)}) copy-start(f32[5,256,768]{2,1,0:T(8,128)} %rel_weights.3) | copy-start | bytes 11796484
  4.5 1.1 copy-start.2
  5.6 0.9 copy-start.4
  6.6 1.0 copy-start.7
  7.6 51.9 %copy-start.1 = (f32[5,256,768]{2,1,0:T(8,128)S(1)}, f32[5,256,768]{2,1,0:T(8,128)}, u32[]{:S(2)}) copy-start(f32[5,256,768]{2,1,0:T(8,128)} %rel_weights.3) | copy-start | bytes 11796484
  7.6 51.9 %copy-start.3 = (f32[256,768]{1,0:T(8,128)S(1)}, f32[256,768]{1,0:T(8,128)}, u32[]{:S(2)}) copy-start(f32[256,768]{1,0:T(8,128)} %self_weight.3) | copy-start | bytes 2359300
  7.6 51.9 %copy-start.5 = (f32[256,256]{1,0:T(8,128)S(1)}, f32[256,256]{1,0:T(8,128)}, u32[]{:S(2)}) copy-start(f32[256,256]{1,0:T(8,128)} %near_cotangent.1) | copy-start | bytes 786436
  59.5 1.2 copy-start.6

commit v4 on v3

--- a/solution.py
+++ b/solution.py
@@ -558,7 +558,7 @@
             shape((relations + 1, out_share, half), f32),
             shape((out_share, part_rows), f32),
         ),
-        in_specs=vmem(5),
+        in_specs=[pl.BlockSpec(memory_space=pltpu.HBM)] * 4 + vmem(1),
         out_specs=tuple(vmem(3)),
         scratch_shapes=[
             pltpu.SemaphoreType.DMA((40,)),

time: 186 us -> 186 us (level)
  no operation moved by 1% of the time
where the time goes in v4:
time: 186 us; the launch traced here: 185 us
  Pallas kernels  172 us (92%)
  local copies, waits for them, and re-layouts  7.31 us (4%)
  other arithmetic  5.53 us (3%)
    pallas_call x1, Pallas kernels, plane_gather(): pl.pallas_call(reduce_kernel, out_shape=(shape((relations, out_share, fea...  103 us
    pallas_call x1, Pallas kernels, plane_gather(): pl.pallas_call(gather_kernel, out_shape=(shape((chunks, parts * seg, LANE...  51.9 us
    pallas_call x1, Pallas kernels, plane_gather(): pl.pallas_call(compute_kernel, out_shape=(shape((out_share, part_rows), f...  16.9 us
    unnamed x17, local copies, waits for them, and re-layouts  7.14 us

profile of v4, /device:TPU:1, one launch (start us, length us, event | category | flops | bytes accessed | tf_op | source)
XLA Modules:
  0.0 185.4 jit_solution(12896452137219565987)
XLA Ops:
  0.6 0.1 pad_add_fusion.me
  0.7 0.8 bitcast_add_fusion.codes
  1.5 0.7 convert_element_type.13
  2.2 0.1 copy.20
  2.3 0.1 convert_element_type.14
  2.4 0.0 copy-start
  2.4 2.1 %copy-done = f32[5,256,768]{2,1,0:T(8,128)S(1)} copy-done((f32[5,256,768]{2,1,0:T(8,128)S(1)}, f32[5,256,768]{2,1,0:T(8,128)}, u32[]{:S(2)}) %copy-start) | copy-done | bytes 3932184
  4.5 0.0 copy-start.2
  4.5 1.1 copy-done.2
  5.6 0.0 copy-start.4
  5.6 0.9 copy-done.4
  6.6 0.0 copy-start.7
  6.6 1.0 copy-done.7
  7.6 0.0 copy-start.1
  7.6 0.0 copy-start.3
  7.6 0.0 copy-start.5
  7.6 51.9 %gather_nodes.1 = (f32[3,4224,128]{2,1,0:T(8,128)S(1)}, f32[6,256,384]{2,1,0:T(8,128)S(1)}, f32[256,256]{1,0:T(8,128)S(1)}) custom-call(f32[128,768]{1,0:T(8,128)S(1)} %copy-done.7, f32[5,256,768]{2,1,0:T(8,128)S(1)} %copy-done, f32[256,768]{1,0:T(8,128)S(1)} %copy-done.2, f32[256,256]{1,0:T(8,128)S(1)} %copy-done.4, f32[8,128]{1,0:T(8,128)S(1)} %pad_bitcast_fusion.mask), custom_call_target="tpu_custom_call" | custom-call | tf_op jit(solution)/shard_map/gather_nodes/pallas_call | solution.py:554
  59.5 0.0 copy-done.1
  59.5 0.0 copy-done.3
  59.5 0.0 copy-done.5
  59.5 0.0 copy-start.6
  59.5 1.2 copy-done.6
  60.7 16.9 %local_products.1 = (f32[256,256]{1,0:T(8,128)S(1)}, f32[256,256]{1,0:T(8,128)S(1)}, f32[3,4096,128]{2,1,0:T(8,128)S(1)}, f32[3,3072,128]{2,1,0:T(8,128)S(1)}) custom-call(s32[5,6]{1,0:T(8,128)S(1)} %bitcast_add_fusion.codes, s32[2]{0:T(128)S(1)} %pad_add_fusion.me, bf16[30,128,128]{2,1,0:T(8,128)(2,1)S(1)} %bitcast.8, ...), custom_call_target="tpu_custom_call" | custom-call | tf_op jit(solution)/shard_map/local_products/pallas_call | solution.py:578
  77.6 103.1 %reduce_grads.1 = (f32[5,256,768]{2,1,0:T(8,128)S(1)}, f32[256,768]{1,0:T(8,128)S(1)}, f32[128,768]{1,0:T(8,128)S(1)}, f32[256,256]{1,0:T(8,128)S(1)}) custom-call(f32[3,4096,128]{2,1,0:T(8,128)S(1)} %get-tuple-element.19.feat_parts, f32[3,3072,128]{2,1,0:T(8,128)S(1)} %get-tuple-element.20.rel_parts, f32[256,256]{1,0:T(8,128)S(1)} %get-tuple-element.21.far_out), custom_call_target="tpu_custom_call" | custom-call | tf_op jit(solution)/shard_map/reduce_grads/pallas_call | solution.py:599
  180.7 0.7 add.22
  181.4 0.9 broadcast_multiply_fusion.1
  182.3 2.3 %broadcast_multiply_fusion = f32[5,256,768]{2,1,0:T(8,128)} fusion(f32[5,256,768]{2,1,0:T(8,128)S(1)} %get-tuple-element.24), kind=kLoop, calls=%fused_computation | loop fusion | flops 983040 | bytes 7864320 | tf_op jit(solution)/shard_map/mul | solution.py:624
  184.6 0.7 copy.35
  (1 shorter events, 0.0 us)
Async XLA Ops:
  2.4 2.1 %copy-start = (f32[5,256,768]{2,1,0:T(8,128)S(1)}, f32[5,256,768]{2,1,0:T(8,128)}, u32[]{:S(2)}) copy-start(f32[5,256,768]{2,1,0:T(8,128)} %rel_weights.3) | copy-start | bytes 11796484
  4.5 1.1 copy-start.2
  5.6 0.9 copy-start.4
  6.6 1.0 copy-start.7
  7.6 51.9 %copy-start.1 = (f32[5,256,768]{2,1,0:T(8,128)S(1)}, f32[5,256,768]{2,1,0:T(8,128)}, u32[]{:S(2)}) copy-start(f32[5,256,768]{2,1,0:T(8,128)} %rel_weights.3) | copy-start | bytes 11796484
  7.6 51.9 %copy-start.3 = (f32[256,768]{1,0:T(8,128)S(1)}, f32[256,768]{1,0:T(8,128)}, u32[]{:S(2)}) copy-start(f32[256,768]{1,0:T(8,128)} %self_weight.3) | copy-start | bytes 2359300
  7.6 51.9 %copy-start.5 = (f32[256,256]{1,0:T(8,128)S(1)}, f32[256,256]{1,0:T(8,128)}, u32[]{:S(2)}) copy-start(f32[256,256]{1,0:T(8,128)} %near_cotangent.1) | copy-start | bytes 786436
  59.5 1.2 copy-start.6

commit v5 on v4

--- a/solution.py
+++ b/solution.py
@@ -299,7 +299,7 @@
 
 def compute_kernel(
     codes, me, tiles, gathered, rel_weights, self_weight, far_weights,
-    near_cotangent, far_cotangent, near_out, far_out, feat_parts, rel_parts, masks, mask_sems,
+    near_cotangent, far_cotangent, mixed, feat_parts, masks, mask_sems,
 ):
     relations, slots = codes.shape
     chunks = gathered.shape[0]
@@ -316,11 +316,8 @@
     ]
     for copy in copies:
         copy.start()
-    near = parts_of(near_cotangent[...])
-    far = parts_of(far_cotangent[...])
     near_t = parts_of(near_cotangent[...].T)
     far_t = parts_of(far_cotangent[...].T)
-    share_rows = out_share // 16
     near_columns = columns(share * half, half)
     feat_parts[...] = jnp.zeros_like(feat_parts)
     for copy in copies:
@@ -329,29 +326,15 @@
     def feat_start(sender):
         return rank_of(sender) * part_rows
 
-    def project(r, z, near_w):
+    def back_through(r, near_w):
         far_w = parts_of(far_weights[r])
-        near_part = product(near_w, z, ((1,), (1,)))
-        far_part = product(far_w, z, ((1,), (1,)))
-        for which, grad in enumerate((near, far)):
-            result = product(grad, z, ((1,), (0,)))
-            for q in range(16):
-                start = (q * 2 + which) * (relations + 1) * share_rows + r * share_rows
-                for k in range(chunks):
-                    rel_parts[k, rows(start, share_rows), :] = result[
-                        q * share_rows : (q + 1) * share_rows, k * LANES : (k + 1) * LANES
-                    ]
-        grad = product(near_t, near_w, ((1,), (0,))) + product(far_t, far_w, ((1,), (0,)))
-        return near_part, far_part, grad
+        return product(near_t, near_w, ((1,), (0,))) + product(far_t, far_w, ((1,), (0,)))
 
     own = jnp.concatenate(
         [gathered[k, rows(rank_of(node) * seg, part_rows), :] for k in range(chunks)], axis=1
     )
-    near_part, far_part, grad = project(
-        relations, parts_of(own), parts_of(self_weight[:, near_columns])
-    )
-    near_out[...] = near_part
-    far_out[...] = far_part
+    mixed[relations] = own
+    grad = back_through(relations, parts_of(self_weight[:, near_columns]))
     for k in range(chunks):
         feat_parts[k, rows(feat_start(node), part_rows), :] = grad[
             :, k * LANES : (k + 1) * LANES
@@ -391,10 +374,8 @@
             )
             places.append((peer, block))
         dense = jnp.concatenate(dense, axis=1)
-        z = parts_of(exact_product(dense, jnp.concatenate(pieces, axis=0), ((1,), (0,))))
-        near_part, far_part, grad = project(r, z, parts_of(rel_weights[r, :, near_columns]))
-        near_out[...] += near_part
-        far_out[...] += far_part
+        mixed[r] = exact_product(dense, jnp.concatenate(pieces, axis=0), ((1,), (0,)))
+        grad = back_through(r, parts_of(rel_weights[r, :, near_columns]))
         back = exact_product(dense, grad, ((0,), (0,)))
         for t, (peer, block) in enumerate(places):
             for k in range(chunks):
@@ -414,8 +395,9 @@
 
 
 def reduce_kernel(
-    feat_parts, rel_parts, far_out, rel_total, self_total, feat_total, got_out,
-    feat_sums, rel_sums, crossed, send_sems, recv_sems, own_sems,
+    feat_parts, mixed, rel_weights, self_weight, far_weights, near_cotangent, far_cotangent,
+    rel_total, self_total, feat_total, got_out, near_out,
+    feat_sums, rel_sums, crossed, rel_parts, far_out, send_sems, recv_sems, own_sems,
 ):
     rank, bits, share, partners, across = place()
     chunks = feat_parts.shape[0]
@@ -426,8 +408,30 @@
     relations = rel_total.shape[0]
     greet(partners + [across])
     sender = Sender(send_sems, recv_sems)
-    out_copy = sender.start(far_out, got_out, across)
     local_copies = []
+    half = chunks * LANES
+    near_columns = columns(share * half, half)
+    share_rows = near_cotangent.shape[0] // 16
+
+    def project(r, near_w):
+        z = parts_of(mixed[r])
+        near_out[...] += product(parts_of(near_w), z, ((1,), (1,)))
+        far_out[...] += product(parts_of(far_weights[r]), z, ((1,), (1,)))
+        for which, grad in enumerate((near_cotangent, far_cotangent)):
+            result = product(parts_of(grad[...]), z, ((1,), (0,)))
+            for q in range(16):
+                start = (q * 2 + which) * (relations + 1) * share_rows + r * share_rows
+                for k in range(chunks):
+                    rel_parts[k, rows(start, share_rows), :] = result[
+                        q * share_rows : (q + 1) * share_rows, k * LANES : (k + 1) * LANES
+                    ]
+
+    def project_some(low, high):
+        def body(r, carry):
+            project(r, rel_weights[r, :, near_columns])
+            return carry
+
+        lax.fori_loop(low, high, body, 0)
 
     def chain(kind, k):
         inputs, sums, seg = (
@@ -512,12 +516,24 @@
                 ]
             yield
 
-    chains = [chain("rel", k) for k in range(chunks)] + [chain("feat", k) for k in range(chunks)]
+    chains = [chain("feat", k) for k in range(chunks)]
+    for one in chains:
+        next(one)
+    near_out[...] = jnp.zeros_like(near_out)
+    far_out[...] = jnp.zeros_like(far_out)
     next(chains[0])
-    active = []
+    project_some(0, 2)
+    next(chains[1])
+    project_some(2, 4)
+    next(chains[2])
+    project_some(4, relations)
+    project(relations, self_weight[:, near_columns])
+    out_copy = sender.start(far_out, got_out, across)
+    active = list(chains)
+    chains = [chain("rel", k) for k in range(chunks)]
+    for one in chains:
+        next(one)
     while chains or active:
-        if len(chains) > 1:
-            next(chains[1])
         if chains:
             active.append(chains.pop(0))
         for one in reversed(list(active)):
@@ -575,16 +591,14 @@
     me = jnp.stack([node, share]).astype(jnp.int32)
     rel_rows = (relations + 1) * out_share // parts
     smem = [pl.BlockSpec(memory_space=pltpu.SMEM)] * 2
-    near_out, far_out, feat_parts, rel_parts = pl.pallas_call(
+    mixed, feat_parts = pl.pallas_call(
         compute_kernel,
         out_shape=(
-            shape((out_share, part_rows), f32),
-            shape((out_share, part_rows), f32),
+            shape((relations + 1, part_rows, half), f32),
             shape((chunks, parts * part_rows, LANES), f32),
-            shape((chunks, parts * 2 * rel_rows, LANES), f32),
         ),
         in_specs=smem + vmem(7),
-        out_specs=tuple(vmem(4)),
+        out_specs=tuple(vmem(2)),
         scratch_shapes=[
             pltpu.SMEM((parts, MASK_ROWS, LANES), f32),
             pltpu.SemaphoreType.DMA((parts,)),
@@ -596,29 +610,32 @@
         tile_values[0].reshape(relations * slots, TILE, TILE),
         gathered, rel_weights, self_weight, far_weights, cotangent, far_cotangent,
     )
-    rel_total, self_total, feat_total, got_out = pl.pallas_call(
+    rel_total, self_total, feat_total, got_out, near_out = pl.pallas_call(
         reduce_kernel,
         out_shape=(
             shape((relations, out_share, features), f32),
             shape((out_share, features), f32),
             shape((own_rows, features), f32),
             shape((out_share, part_rows), f32),
+            shape((out_share, part_rows), f32),
         ),
-        in_specs=vmem(3),
-        out_specs=tuple(vmem(4)),
+        in_specs=vmem(7),
+        out_specs=tuple(vmem(5)),
         scratch_shapes=[
             pltpu.VMEM((chunks, 15 * part_rows, LANES), f32),
             pltpu.VMEM((chunks, 15 * 2 * rel_rows, LANES), f32),
             pltpu.VMEM((chunks, rel_rows, LANES), f32),
+            pltpu.VMEM((chunks, parts * 2 * rel_rows, LANES), f32),
+            pltpu.VMEM((out_share, part_rows), f32),
             pltpu.SemaphoreType.DMA((96,)),
             pltpu.SemaphoreType.DMA((96,)),
             pltpu.SemaphoreType.DMA((2 * chunks,)),
         ],
         compiler_params=pltpu.CompilerParams(
-            collective_id=1, has_side_effects=True, vmem_limit_bytes=28 * MIB
+            collective_id=1, has_side_effects=True, vmem_limit_bytes=34 * MIB
         ),
         name="reduce_grads",
-    )(feat_parts, rel_parts, far_out)
+    )(feat_parts, mixed, rel_weights, self_weight, far_weights, cotangent, far_cotangent)
     layer_out = near_out + got_out
     factor = float(part_rows * parts) ** (-0.5)
     return (layer_out, feat_total, rel_total * factor, self_total * factor)

time: 186 us -> 204 us (1.097)
  Pallas kernels: 172 us -> 188 us
  local copies, waits for them, and re-layouts: 7.31 us -> 9.96 us
    pallas_call x1, Pallas kernels: 103 us -> 125 us  [plane_gather(): pl.pallas_call(reduce_kernel, out_shape=(shape((relations, out_share, fea...]
    pallas_call x1, Pallas kernels: 16.9 us -> 11.2 us  [plane_gather(): pl.pallas_call(compute_kernel, out_shape=(shape((relations + 1, part_rows...]
    unnamed x17 -> x19, local copies, waits for them, and re-layouts: 7.14 us -> 9.79 us
where the time goes in v5:
time: 204 us
  Pallas kernels  188 us (92%)
  local copies, waits for them, and re-layouts  9.96 us (5%)
  other arithmetic  5.53 us (3%)
    pallas_call x1, Pallas kernels, plane_gather(): pl.pallas_call(reduce_kernel, out_shape=(shape((relations, out_share, fea...  125 us
    pallas_call x1, Pallas kernels, plane_gather(): pl.pallas_call(gather_kernel, out_shape=(shape((chunks, parts * seg, LANE...  51.9 us
    pallas_call x1, Pallas kernels, plane_gather(): pl.pallas_call(compute_kernel, out_shape=(shape((relations + 1, part_rows...  11.2 us
    unnamed x19, local copies, waits for them, and re-layouts  9.79 us

profile of v5, /device:TPU:1, one launch (start us, length us, event | category | flops | bytes accessed | tf_op | source)
XLA Modules:
  0.0 203.9 jit_solution(855344267289767632)
XLA Ops:
  0.6 0.1 pad_add_fusion.me
  0.7 0.8 bitcast_add_fusion.codes
  1.5 0.7 convert_element_type.13
  2.2 0.1 copy.20
  2.3 0.1 convert_element_type.14
  2.4 0.0 copy-start
  2.4 2.1 %copy-done = f32[5,256,768]{2,1,0:T(8,128)S(1)} copy-done((f32[5,256,768]{2,1,0:T(8,128)S(1)}, f32[5,256,768]{2,1,0:T(8,128)}, u32[]{:S(2)}) %copy-start) | copy-done | bytes 3932184
  4.5 0.0 copy-start.2
  4.5 1.1 copy-done.2
  5.6 0.0 copy-start.5
  5.6 0.9 copy-done.5
  6.6 0.0 copy-start.8
  6.6 1.0 copy-done.8
  7.6 0.0 copy-start.1
  7.6 0.0 copy-start.3
  7.6 0.0 copy-start.6
  7.6 51.9 %gather_nodes.1 = (f32[3,4224,128]{2,1,0:T(8,128)S(1)}, f32[6,256,384]{2,1,0:T(8,128)S(1)}, f32[256,256]{1,0:T(8,128)S(1)}) custom-call(f32[128,768]{1,0:T(8,128)S(1)} %copy-done.8, f32[5,256,768]{2,1,0:T(8,128)S(1)} %copy-done, f32[256,768]{1,0:T(8,128)S(1)} %copy-done.2, f32[256,256]{1,0:T(8,128)S(1)} %copy-done.5, f32[8,128]{1,0:T(8,128)S(1)} %pad_bitcast_fusion.mask), custom_call_target="tpu_custom_call" | custom-call | tf_op jit(solution)/shard_map/gather_nodes/pallas_call | solution.py:570
  59.5 0.0 copy-done.1
  59.5 0.0 copy-done.3
  59.5 0.0 copy-done.6
  59.5 0.0 copy-start.7
  59.5 1.2 copy-done.7
  60.7 11.2 %local_products.1 = (f32[6,256,384]{2,1,0:T(8,128)S(1)}, f32[3,4096,128]{2,1,0:T(8,128)S(1)}) custom-call(s32[5,6]{1,0:T(8,128)S(1)} %bitcast_add_fusion.codes, s32[2]{0:T(128)S(1)} %pad_add_fusion.me, bf16[30,128,128]{2,1,0:T(8,128)(2,1)S(1)} %bitcast.8, f32[3,4224,128]{2,1,0:T(8,128)S(1)} %get-tuple-element.14.gathered, f32[5,256,768]{2,1,0:T(8,128)S(1)} %copy-done.1, ...), custom_call_target="tpu_custom_call" | custom-call | tf_op jit(solution)/shard_map/local_products/pallas_call | solution.py:594
  71.9 0.0 copy-start.4
  71.9 2.6 %copy-done.4 = f32[3,4096,128]{2,1,0:T(8,128)} copy-done((f32[3,4096,128]{2,1,0:T(8,128)}, f32[3,4096,128]{2,1,0:T(8,128)S(1)}, u32[]{:S(2)}) %copy-start.4) | copy-done | bytes 6291480
  74.6 124.6 %reduce_grads.1 = (f32[5,256,768]{2,1,0:T(8,128)S(1)}, f32[256,768]{1,0:T(8,128)S(1)}, f32[128,768]{1,0:T(8,128)S(1)}, f32[256,256]{1,0:T(8,128)S(1)}, f32[256,256]{1,0:T(8,128)S(1)}) custom-call(f32[3,4096,128]{2,1,0:T(8,128)} %copy-done.4, f32[6,256,384]{2,1,0:T(8,128)S(1)} %get-tuple-element.18.mixed, f32[5,256,768]{2,1,0:T(8,128)S(1)} %copy-done.1, ...), custom_call_target="tpu_custom_call" | custom-call | tf_op jit(solution)/shard_map/reduce_grads/pallas_call | solution.py:613
  199.2 0.7 add.22
  199.9 0.9 broadcast_multiply_fusion.1
  200.9 2.3 %broadcast_multiply_fusion = f32[5,256,768]{2,1,0:T(8,128)} fusion(f32[5,256,768]{2,1,0:T(8,128)S(1)} %get-tuple-element.22), kind=kLoop, calls=%fused_computation | loop fusion | flops 983040 | bytes 7864320 | tf_op jit(solution)/shard_map/mul | solution.py:641
  203.2 0.7 copy.35
  (1 shorter events, 0.0 us)
Async XLA Ops:
  2.4 2.1 %copy-start = (f32[5,256,768]{2,1,0:T(8,128)S(1)}, f32[5,256,768]{2,1,0:T(8,128)}, u32[]{:S(2)}) copy-start(f32[5,256,768]{2,1,0:T(8,128)} %rel_weights.5) | copy-start | bytes 11796484
  4.5 1.1 copy-start.2
  5.6 0.9 copy-start.5
  6.6 1.0 copy-start.8
  7.6 51.9 %copy-start.1 = (f32[5,256,768]{2,1,0:T(8,128)S(1)}, f32[5,256,768]{2,1,0:T(8,128)}, u32[]{:S(2)}) copy-start(f32[5,256,768]{2,1,0:T(8,128)} %rel_weights.5) | copy-start | bytes 11796484
  7.6 51.9 %copy-start.3 = (f32[256,768]{1,0:T(8,128)S(1)}, f32[256,768]{1,0:T(8,128)}, u32[]{:S(2)}) copy-start(f32[256,768]{1,0:T(8,128)} %self_weight.5) | copy-start | bytes 2359300
  7.6 51.9 %copy-start.6 = (f32[256,256]{1,0:T(8,128)S(1)}, f32[256,256]{1,0:T(8,128)}, u32[]{:S(2)}) copy-start(f32[256,256]{1,0:T(8,128)} %near_cotangent.3) | copy-start | bytes 786436
  59.5 1.2 copy-start.7
  71.9 2.7 %copy-start.4 = (f32[3,4096,128]{2,1,0:T(8,128)}, f32[3,4096,128]{2,1,0:T(8,128)S(1)}, u32[]{:S(2)}) copy-start(f32[3,4096,128]{2,1,0:T(8,128)S(1)} %get-tuple-element.17.feat_parts) | copy-start | bytes 18874372
